TPU v7x, 128 devices: a whole 4x4x4 slice. The times are simulated.
128 devices in a mesh: dp: 4 (over z), expert: 32 (over x, y, core).
Axes of the slice: x: 4, y: 4, z: 4, core: 2. Of those that a mesh axis runs over, the one named last changes fastest.
Arguments:
- attn_prefill: bfloat16 [15360, 2048], P(('dp', 'expert')), may hold values from -6 to 6
- decode_held: bfloat16 [512, 2048], P(('dp', 'expert')), may hold values from -6 to 6
- decode_source: int32 [512], P(('dp', 'expert')), may hold values from 0 to 15, as said below
- residual: bfloat16 [15872, 2048], P(('dp', 'expert')), may hold values from -6 to 6
- live_rows: int32 [128], P(('dp', 'expert')), may hold values from 1 to 120, 11520 in all
- expert_ids: int32 [15872, 6], P(('dp', 'expert')), may hold values from 0 to 31, all different within a row; in each aligned block of 124 rows (0 to 123, 124 to 247, ...) at most 24 rows name the same one
- replica_pick: int32 [128, 32], P(('dp', 'expert')), may hold values from 0 to 3
- w_out: bfloat16 [2048, 2048], P(None, 'dp'), may hold values from -0.125 to 0.125
- norm_gain: float32 [2048], replicated, may hold values from 0.5 to 1.5
- router: bfloat16 [2048, 32], replicated, may hold values from -8 to 8
- exp_gate: bfloat16 [32, 2048, 1408], P('expert'), may hold values from -0.125 to 0.125
- exp_up: bfloat16 [32, 2048, 1408], P('expert'), may hold values from -0.125 to 0.125
- exp_down: bfloat16 [32, 1408, 2048], P('expert'), may hold values from -0.15625 to 0.15625
- shared_gate: bfloat16 [1408, 2048], P('dp'), may hold values from -0.125 to 0.125
- shared_up: bfloat16 [1408, 2048], P('dp'), may hold values from -0.125 to 0.125
- shared_down: bfloat16 [1408, 2048], P('dp'), may hold values from -0.15625 to 0.15625
Outputs:
- out: bfloat16 [15872, 2048], P(('dp', 'expert'))
- copy_rows: int32 [128], P(('dp', 'expert'))
Inputs may be any that keep to these rules, and one draw needn't show every extreme that they name: `expert_ids`: each row names 6 different experts; within the rows of one device no expert is named by more than 24 rows, and in some or all devices one expert is named by exactly 24 rows. `live_rows`: the values sum to 11520, and the largest is exactly 120. `decode_source`: for each index c of expert, the entries of the devices (r, c), taken in order of r, are a permutation of 0 .. 15.
All inputs are finite; a program needn't handle non-finite values.
Results may differ from a plain program's by a relative error of at most 0.01.
Values may be sent and summed in bfloat16 or wider, within the bound.
A program may use at most 128 MiB of HBM per device.

v0:
```python
import jax
import jax.numpy as jnp
from jax import lax
from jax.sharding import PartitionSpec as P

EPSILON = 1e-06


def expert_apply(arrived_pair, exp_gate, exp_up, exp_down):
    arrived, arrived_marks = arrived_pair
    gate_part = jnp.einsum("sekd,edf->sekf", arrived, exp_gate, preferred_element_type=jnp.float32)
    up_part = jnp.einsum("sekd,edf->sekf", arrived, exp_up, preferred_element_type=jnp.float32)
    expert_inner = (jax.nn.silu(gate_part) * up_part).astype(jnp.bfloat16)
    expert_out = jnp.einsum(
        "sekf,efd->sekd", expert_inner, exp_down, preferred_element_type=jnp.float32
    ).astype(jnp.bfloat16)
    return (expert_out, arrived_marks)


def body(
    attn_prefill,
    decode_held,
    decode_source,
    residual,
    live_rows,
    expert_ids,
    replica_pick,
    w_out,
    norm_gain,
    router,
    exp_gate,
    exp_up,
    exp_down,
    shared_gate,
    shared_up,
    shared_down,
):
    dp_count = lax.axis_size("dp")
    column_count = lax.axis_size("expert")
    device_count = dp_count * column_count
    prefill_count = attn_prefill.shape[0]
    feature_width = attn_prefill.shape[1]
    expert_total = router.shape[1]
    top_count = expert_ids.shape[1]
    held_experts = exp_gate.shape[0]
    row_count = residual.shape[0]
    most_rows = dp_count * (row_count * top_count // (dp_count * expert_total) + 1)
    slot_count = most_rows // dp_count
    slot_block = held_experts * slot_count
    contract = (((1,), (1,)), ((), ()))
    group_rows = lax.all_gather(decode_held, "dp", axis=0, tiled=True)
    decode_rows = jnp.take(group_rows, decode_source, axis=0)
    attn_all = jnp.concatenate([attn_prefill, decode_rows], axis=0)
    proj_columns = jnp.dot(
        lax.all_gather(attn_all, "dp", axis=0, tiled=True),
        w_out,
        preferred_element_type=jnp.float32,
    ).astype(jnp.bfloat16)
    projected = lax.all_to_all(proj_columns, "dp", split_axis=0, concat_axis=1, tiled=True)
    hidden = residual.astype(jnp.float32) + projected.astype(jnp.float32)
    inverse_rms = lax.rsqrt(jnp.mean(hidden * hidden, axis=1, keepdims=True) + EPSILON)
    normed = (hidden * inverse_rms * norm_gain[None, :]).astype(jnp.bfloat16)
    router_logits = jnp.dot(normed, router, preferred_element_type=jnp.float32)
    expert_probs = jax.nn.softmax(router_logits, axis=1)
    row_index = jnp.arange(row_count)
    row_live = (row_index < live_rows[0]) | (row_index >= prefill_count)
    expert_match = (
        expert_ids[:, :, None] == jnp.arange(expert_total, dtype=jnp.int32)[None, None, :]
    )
    choice_gates = jnp.sum(
        jnp.where(expert_match, expert_probs[:, None, :], 0.0), axis=2
    ) * row_live[:, None].astype(jnp.float32)
    flat_match = expert_match.reshape(row_count * top_count, expert_total).astype(jnp.int32)
    choice_live = jnp.repeat(row_live, top_count)
    choice_hits = flat_match * choice_live[:, None].astype(jnp.int32)
    choice_rank = jnp.sum((jnp.cumsum(choice_hits, axis=0) - choice_hits) * choice_hits, axis=1)
    flat_ids = expert_ids.reshape(row_count * top_count)
    replica_row = jnp.sum(flat_match * replica_pick[0][None, :], axis=1)
    copy_row = (replica_row + choice_rank) % dp_count
    destination = copy_row * column_count + flat_ids // held_experts
    slot_index = (
        destination * slot_block + flat_ids % held_experts * slot_count + choice_rank // dp_count
    )
    slot_index = jnp.where(choice_live, slot_index, device_count * slot_block)
    source_rows = jnp.repeat(normed, top_count, axis=0)
    outgoing = (
        jnp.zeros((device_count * slot_block, feature_width), jnp.bfloat16)
        .at[slot_index]
        .set(source_rows, mode="drop")
    )
    slot_marks = (
        jnp.zeros((device_count * slot_block,), jnp.int32).at[slot_index].set(1, mode="drop")
    )
    outgoing = outgoing.reshape(device_count, held_experts, slot_count, feature_width)
    slot_marks = slot_marks.reshape(device_count, held_experts, slot_count)
    expert_out, arrived_marks = expert_apply(
        (
            lax.all_to_all(outgoing, ("dp", "expert"), split_axis=0, concat_axis=0, tiled=True),
            lax.all_to_all(slot_marks, ("dp", "expert"), split_axis=0, concat_axis=0, tiled=True),
        ),
        exp_gate,
        exp_up,
        exp_down,
    )
    returned = lax.all_to_all(expert_out, ("dp", "expert"), split_axis=0, concat_axis=0, tiled=True)
    row_piece = lax.all_gather(normed, "dp", axis=0, tiled=True)
    gate_part = lax.dot_general(
        row_piece, shared_gate, contract, preferred_element_type=jnp.float32
    )
    up_part = lax.dot_general(row_piece, shared_up, contract, preferred_element_type=jnp.float32)
    shared_inner = (jax.nn.silu(gate_part) * up_part).astype(jnp.bfloat16)
    shared_out = lax.psum_scatter(
        jnp.dot(shared_inner, shared_down, preferred_element_type=jnp.float32).astype(jnp.bfloat16),
        "dp",
        scatter_dimension=0,
        tiled=True,
    ).astype(jnp.float32)
    returned = returned.reshape(device_count * slot_block, feature_width)
    fetched = jnp.take(
        returned, jnp.minimum(slot_index, device_count * slot_block - 1), axis=0
    ).reshape(row_count, top_count, feature_width)
    routed = jnp.sum(choice_gates[:, :, None] * fetched.astype(jnp.float32), axis=1)
    out = (hidden + shared_out + routed).astype(jnp.bfloat16)
    copy_rows = jnp.sum(arrived_marks).reshape(1).astype(jnp.int32)
    return (out, copy_rows)


def solution(mesh):
    placed = (
        P(("dp", "expert"), None),
        P(("dp", "expert"), None),
        P(("dp", "expert")),
        P(("dp", "expert"), None),
        P(("dp", "expert")),
        P(("dp", "expert"), None),
        P(("dp", "expert"), None),
        P(None, "dp"),
        P(),
        P(),
        P("expert", None, None),
        P("expert", None, None),
        P("expert", None, None),
        P("dp", None),
        P("dp", None),
        P("dp", None),
    )
    return jax.shard_map(
        body,
        mesh=mesh,
        in_specs=placed,
        out_specs=(P(("dp", "expert"), None), P(("dp", "expert"))),
        check_vma=False,
    )
```

profile of v0, /device:TPU:1, one launch (start us, length us, event | category | flops | bytes accessed | tf_op | source)
XLA Modules:
  0.0 335.5 jit_solution(3082956291351788636)
XLA Ops:
  8.7 11.5 %all-gather = bf16[4,4,2048]{2,1,0:T(4,128)(2,1)S(1)} all-gather(bf16[1,4,2048]{2,1,0:T(4,128)(2,1)} %bitcast.127), channel_id=1, replica_groups=mesh['dp'=4,'expert'=32] {'dp'}, dimensions={0}, use_global_device_ids=true | all-gather | bytes 81920 | tf_op jit(solution)/shard_map/all_gather | solution.py:51
  20.9 1.9 maximum_bitcast_fusion
  24.8 1.7 reduce-window.6
  27.1 30.7 %all-gather.6.cloned.1.call-done = bf16[4,124,2048]{2,1,0:T(8,128)(2,1)} async-done(((bf16[1,124,2048]{2,1,0:T(8,128)(2,1)}), bf16[4,124,2048]{2,1,0:T(8,128)(2,1)}) %all-gather.6.cloned.1.call-update) | async-done | bytes 2031632 | tf_op jit(solution)/shard_map/all_gather | solution.py:55
  57.8 2.7 reshape.337
  60.5 2.8 convolution_convert_fusion.1
  64.2 3.5 %all-to-all-start = ((bf16[4,124,512]{2,1,0:T(8,128)(2,1)}), bf16[4,124,512]{2,1,0:T(8,128)(2,1)S(1)}, u32[]{:S(2)}, u32[]{:S(2)}) async-start(bf16[4,124,512]{2,1,0:T(8,128)(2,1)} %all_to_all.19), calls=%async_computation | async-start | bytes 1048576 | tf_op jit(solution)/shard_map/all_to_all | solution.py:59
  68.0 4.1 %scatter_custom_fusion.1 = s32[768]{0:T(1024)S(1)} fusion(s32[744]{0:T(1024)S(1)} %get-tuple-element.7, s32[744]{0:T(1024)S(1)} %broadcast.450, s32[]{:T(128)} %constant.97.clone.1), kind=kCustom, calls=%fused_computation.97 | custom fusion | bytes 3076 | tf_op jit(solution)/shard_map/scatter | solution.py:92
  72.8 3.7 %all-to-all-done = bf16[4,124,512]{2,1,0:T(8,128)(2,1)S(1)} async-done(((bf16[4,124,512]{2,1,0:T(8,128)(2,1)}), bf16[4,124,512]{2,1,0:T(8,128)(2,1)S(1)}, u32[]{:S(2)}, u32[]{:S(2)}) %all-to-all-start) | async-done | bytes 507936 | tf_op jit(solution)/shard_map/all_to_all | solution.py:59
  76.5 8.4 %all-to-all-start.3 = ((s32[128,1,6]{2,1,0:T(1,128)}), s32[128,1,6]{2,1,0:T(1,128)S(1)}, u32[]{:S(2)}, u32[]{:S(2)}) async-start(s32[128,1,6]{2,1,0:T(1,128)} %bitcast.28), calls=%async_computation.3 | async-start | bytes 131072 | tf_op jit(solution)/shard_map/all_to_all | solution.py:99
  87.1 2.6 broadcast_in_dim.77
  89.7 6.1 %reshape.321 = bf16[744,2048]{1,0:T(8,128)(2,1)} reshape(bf16[124,6,2048]{2,1,0:T(8,128)(2,1)} %broadcast_in_dim.77) | data formatting | bytes 6094848 | tf_op jit(solution)/shard_map/reshape | solution.py:85
  95.8 8.8 %scatter_custom_fusion = bf16[768,2048]{1,0:T(8,128)(2,1)S(1)} fusion(s32[744]{0:T(1024)S(1)} %get-tuple-element.7, bf16[744,2048]{1,0:T(8,128)(2,1)} %reshape.321, bf16[]{:T(256)} %constant.116.clone.1), kind=kCustom, calls=%fused_computation.26 | custom fusion | bytes 3146240 | tf_op jit(solution)/shard_map/scatter | solution.py:89
  104.7 2.9 reshape.291
  107.6 10.2 %all-to-all-start.1 = ((bf16[128,1,6,2048]{3,2,1,0:T(8,128)(2,1)}), bf16[128,1,6,2048]{3,2,1,0:T(8,128)(2,1)}, u32[]{:S(2)}, u32[]{:S(2)}) async-start(bf16[128,1,6,2048]{3,2,1,0:T(8,128)(2,1)} %bitcast.124), calls=%async_computation.1 | async-start | bytes 8388608 | tf_op jit(solution)/shard_map/all_to_all | solution.py:98
  121.7 61.7 %all-gather.8.cloned.1.call-done = bf16[4,124,2048]{2,1,0:T(8,128)(2,1)} async-done(((bf16[1,124,2048]{2,1,0:T(8,128)(2,1)}), bf16[4,124,2048]{2,1,0:T(8,128)(2,1)}) %all-gather.8.cloned.1.call-update) | async-done | bytes 2031632 | tf_op jit(solution)/shard_map/all_gather | solution.py:106
  183.5 2.8 reshape.339
  186.2 11.2 %fusion.3 = f32[128,6,1408]{2,0,1:T(8,128)} fusion(bf16[1,2048,1408]{2,1,0:T(8,128)(2,1)} %param.27, bf16[128,1,6,2048]{3,2,1,0:T(8,128)(2,1)} %all-to-all-done.1), kind=kOutput, calls=%fused_computation.7 | convolution fusion | flops 4429185024 | bytes 13238272 | tf_op jit(solution)/shard_map/sekd,edf->sekf/dot_general | solution.py:12
  197.4 18.9 %fusion.18 = bf16[128,1,6,2048]{3,0,2,1:T(8,128)(2,1)S(1)} fusion(bf16[1,1408,2048]{2,1,0:T(8,128)(2,1)} %param.28, f32[128,6,1408]{2,0,1:T(8,128)} %fusion.3, bf16[1,2048,1408]{2,1,0:T(8,128)(2,1)} %param.26, bf16[128,1,6,2048]{3,2,1,0:T(8,128)(2,1)} %all-to-all-done.1), kind=kOutput, calls=%fused_computation.21 | convolution fusion | flops 8866430976 | bytes 22151168 | tf_op jit(solution)/shard_map/sekf,efd->sekd/dot_general | solution.py:14
  216.2 3.8 %copy.132 = bf16[128,1,6,2048]{3,2,1,0:T(8,128)(2,1)} copy(bf16[128,1,6,2048]{3,0,2,1:T(8,128)(2,1)S(1)} %fusion.18) | data formatting | bytes 6291456 | tf_op jit(solution)/shard_map/convert_element_type | solution.py:16
  220.1 8.1 %all-to-all-start.2 = ((bf16[128,1,6,2048]{3,2,1,0:T(8,128)(2,1)}), bf16[128,1,6,2048]{3,2,1,0:T(8,128)(2,1)}, u32[]{:S(2)}, u32[]{:S(2)}) async-start(bf16[128,1,6,2048]{3,2,1,0:T(8,128)(2,1)} %copy.132), calls=%async_computation.2 | async-start | bytes 8388608 | tf_op jit(solution)/shard_map/all_to_all | solution.py:105
  228.2 3.2 fusion.61
  231.4 4.8 %convolution_convert_fusion = bf16[496,2048]{1,0:T(8,128)(2,1)S(1)} fusion(bf16[352,2048]{1,0:T(8,128)(2,1)} %param.31, bf16[496,2048]{1,0:T(8,128)(2,1)} %reshape.339, bf16[352,2048]{1,0:T(8,128)(2,1)} %param.30, f32[496,352]{0,1:T(8,128)} %fusion.61), kind=kOutput, calls=%fused_computation.23 | convolution fusion | flops 1432321024 | bytes 7645184 | tf_op jit(solution)/shard_map/dot_general | solution.py:113
  236.2 63.0 %fusion = bf16[128,2048]{1,0:T(8,128)(2,1)S(1)} fusion(bf16[496,2048]{1,0:T(8,128)(2,1)S(1)} %convolution_convert_fusion), kind=kCustom, calls=%all-reduce-scatter | all-reduce-scatter fusion | flops 1048577 | bytes 2556416
  299.2 1.3 collective-permute-start
  300.6 1.2 collective-permute-done
  301.8 4.3 %concatenate.4 = bf16[140,2048]{1,0:T(8,128)(2,1)} concatenate(bf16[12,2048]{1,0:T(8,128)(2,1)S(1)} %collective-permute-done, bf16[128,2048]{1,0:T(8,128)(2,1)S(1)} %fusion), dimensions={0} | concatenate | bytes 1146880
  306.0 4.9 %reshape.297 = bf16[768,2048]{1,0:T(8,128)(2,1)S(1)} reshape(bf16[128,1,6,2048]{3,2,1,0:T(8,128)(2,1)} %all-to-all-done.2) | data formatting | bytes 6291456 | tf_op jit(solution)/shard_map/reshape | solution.py:118
  310.9 4.3 %gather_fusion.1 = bf16[744,2048]{1,0:T(8,128)(2,1)} fusion(bf16[768,2048]{1,0:T(8,128)(2,1)S(1)} %reshape.297, s32[1024]{0:T(1024)S(1)} %pad_clamp_fusion), kind=kCustom, calls=%fused_computation.1 | custom fusion | bytes 6097824 | tf_op jit(solution)/shard_map/jit(_take)/gather | solution.py:119
  315.2 6.2 %gather.12 = bf16[124,6,2048]{2,1,0:T(8,128)(2,1)} reshape(bf16[744,2048]{1,0:T(8,128)(2,1)} %gather_fusion.1) | data formatting | bytes 6094848 | tf_op jit(solution)/shard_map/jit(_take)/gather | solution.py:119
  321.4 6.1 %multiply_reduce_fusion = f32[124,2048]{1,0:T(8,128)S(1)} fusion(bf16[124,6,2048]{2,1,0:T(8,128)(2,1)} %gather.12, f32[124,6]{1,0:T(8,128)S(1)} %copy.117, pred[124,6]{1,0:T(8,128)(4,1)S(1)} %copy.127), kind=kLoop, calls=%fused_computation.4 | loop fusion | flops 5840896 | bytes 4066952 | tf_op jit(solution)/shard_map/reduce_sum | solution.py:122
  327.5 1.1 add_convert_fusion
  (84 shorter events, 11.3 us)
Async XLA Ops:
  7.2 53.4 %copy-start = (bf16[2048,512]{1,0:T(8,128)(2,1)S(1)}, bf16[2048,512]{1,0:T(8,128)(2,1)}, u32[]{:S(2)}) copy-start(bf16[2048,512]{1,0:T(8,128)(2,1)} %param.23) | copy-start | bytes 6291460
  7.2 50.6 %all-gather.6.cloned.1.call-start = ((), (), s32[]{:S(2)}) async-start(), calls=%async_computation.4 | async-start | bytes 2621440 | tf_op jit(solution)/shard_map/all_gather | solution.py:55
  60.5 7.3 %copy-start.13 = (s32[1,32]{1,0:T(1,128)S(1)}, s32[1,32]{1,0:T(1,128)}, u32[]{:S(2)}) copy-start(s32[1,32]{1,0:T(1,128)} %param.22) | copy-start | bytes 388
  64.2 12.3 %all-to-all-start = ((bf16[4,124,512]{2,1,0:T(8,128)(2,1)}), bf16[4,124,512]{2,1,0:T(8,128)(2,1)S(1)}, u32[]{:S(2)}, u32[]{:S(2)}) async-start(bf16[4,124,512]{2,1,0:T(8,128)(2,1)} %all_to_all.19), calls=%async_computation | async-start | bytes 1048576 | tf_op jit(solution)/shard_map/all_to_all | solution.py:59
  67.7 18.2 %copy-start.6 = (bf16[124,2048]{1,0:T(8,128)(2,1)S(1)}, bf16[124,2048]{1,0:T(8,128)(2,1)}, u32[]{:S(2)}) copy-start(bf16[124,2048]{1,0:T(8,128)(2,1)} %param.19) | copy-start | bytes 1523716
  76.5 31.0 %all-to-all-start.3 = ((s32[128,1,6]{2,1,0:T(1,128)}), s32[128,1,6]{2,1,0:T(1,128)S(1)}, u32[]{:S(2)}, u32[]{:S(2)}) async-start(s32[128,1,6]{2,1,0:T(1,128)} %bitcast.28), calls=%async_computation.3 | async-start | bytes 131072 | tf_op jit(solution)/shard_map/all_to_all | solution.py:99
  85.1 1.0 copy-start.12
  85.9 3.8 %copy-start.2 = (f32[124,2048]{1,0:T(8,128)}, f32[124,2048]{1,0:T(8,128)S(1)}, u32[]{:S(2)}) copy-start(f32[124,2048]{1,0:T(8,128)S(1)} %copy.116) | copy-start | bytes 3047428
  86.3 0.8 copy-start.4
  107.6 11.4 %copy-start.11 = (s32[124,6]{0,1:T(8,128)S(1)}, s32[124,6]{0,1:T(8,128)}, u32[]{:S(2)}) copy-start(s32[124,6]{0,1:T(8,128)} %param.21) | copy-start | bytes 8932
  107.6 11.6 %copy-start.14 = (u32[128]{0:T(128)S(1)}, u32[128]{0:T(128)}, u32[]{:S(2)}) copy-start(u32[128]{0:T(128)} %constant.131) | copy-start | bytes 1540
  107.6 13.8 %copy-start.5 = (bf16[124,2048]{1,0:T(8,128)(2,1)S(1)}, bf16[124,2048]{1,0:T(8,128)(2,1)}, u32[]{:S(2)}) copy-start(bf16[124,2048]{1,0:T(8,128)(2,1)} %copy-done.4) | copy-start | bytes 1523716
  107.6 13.8 %copy-start.10 = (bf16[2048,32]{0,1:T(8,128)(2,1)S(1)}, bf16[2048,32]{0,1:T(8,128)(2,1)}, u32[]{:S(2)}) copy-start(bf16[2048,32]{0,1:T(8,128)(2,1)} %param.25) | copy-start | bytes 393220
  107.6 78.7 %all-to-all-start.1 = ((bf16[128,1,6,2048]{3,2,1,0:T(8,128)(2,1)}), bf16[128,1,6,2048]{3,2,1,0:T(8,128)(2,1)}, u32[]{:S(2)}, u32[]{:S(2)}) async-start(bf16[128,1,6,2048]{3,2,1,0:T(8,128)(2,1)} %bitcast.124), calls=%async_computation.1 | async-start | bytes 8388608 | tf_op jit(solution)/shard_map/all_to_all | solution.py:98
  117.8 65.7 %all-gather.8.cloned.1.call-start = ((), (), s32[]{:S(2)}) async-start(), calls=%async_computation.5 | async-start | bytes 2621440 | tf_op jit(solution)/shard_map/all_gather | solution.py:106
  220.1 8.1 %copy-start.9 = (bf16[496,2048]{1,0:T(8,128)(2,1)S(1)}, bf16[496,2048]{1,0:T(8,128)(2,1)}, u32[]{:S(2)}) copy-start(bf16[496,2048]{1,0:T(8,128)(2,1)} %reshape.339) | copy-start | bytes 6094852
  220.1 85.9 %all-to-all-start.2 = ((bf16[128,1,6,2048]{3,2,1,0:T(8,128)(2,1)}), bf16[128,1,6,2048]{3,2,1,0:T(8,128)(2,1)}, u32[]{:S(2)}, u32[]{:S(2)}) async-start(bf16[128,1,6,2048]{3,2,1,0:T(8,128)(2,1)} %copy.132), calls=%async_computation.2 | async-start | bytes 8388608 | tf_op jit(solution)/shard_map/all_to_all | solution.py:105
  299.2 2.6 collective-permute-start
  315.2 13.4 %copy-start.1 = (bf16[2048,512]{1,0:T(8,128)(2,1)S(1)}, bf16[2048,512]{1,0:T(8,128)(2,1)}, u32[]{:S(2)}) copy-start(bf16[2048,512]{1,0:T(8,128)(2,1)} %param.23) | copy-start | bytes 6291460
  321.4 6.1 %copy-start.3 = (f32[124,2048]{1,0:T(8,128)S(1)}, f32[124,2048]{1,0:T(8,128)}, u32[]{:S(2)}) copy-start(f32[124,2048]{1,0:T(8,128)} %copy-done.2) | copy-start | bytes 3047428
  321.4 6.1 %copy-start.7 = (bf16[124,2048]{1,0:T(8,128)(2,1)S(1)}, bf16[124,2048]{1,0:T(8,128)(2,1)}, u32[]{:S(2)}) copy-start(bf16[124,2048]{1,0:T(8,128)(2,1)} %param.19) | copy-start | bytes 1523716
  321.4 6.1 %copy-start.8 = (bf16[140,2048]{1,0:T(8,128)(2,1)S(1)}, bf16[140,2048]{1,0:T(8,128)(2,1)}, u32[]{:S(2)}) copy-start(bf16[140,2048]{1,0:T(8,128)(2,1)} %concatenate.4) | copy-start | bytes 1720324
Sparse Core Ops, SparseCore 0:
  22.9 34.8 all-gather.5
  120.9 62.5 all-gather.7
where the time goes:
time: 337 us; the launch traced here: 335 us
  waiting for transfers between devices  98 us (29%)
  blocking collectives  74.5 us (22%)
  local copies, waits for them, and re-layouts  60.4 us (18%)
  matrix products  41 us (12%)
  starting transfers between devices  31.6 us (9%)
  between operations  15.8 us (5%)
  other arithmetic  14.1 us (4%)
    unnamed x1, blocking collectives  63 us
    all_gather x1, waiting for transfers between devices, body(): row_piece = lax.all_gather(normed, 'dp', axis=0, tiled=True)  61.7 us
    all_gather x1, waiting for transfers between devices, body(): lax.all_gather(attn_all, 'dp', axis=0, tiled=True)  30.7 us
    dot_general x1, matrix products, expert_apply(): jnp.einsum('sekf,efd->sekd', expert_inner, exp_down, preferred_element_ty...  18.9 us
    unnamed x37, local copies, waits for them, and re-layouts  12.1 us
    all_gather x1, blocking collectives, body(): group_rows = lax.all_gather(decode_held, 'dp', axis=0, tiled=True)  11.5 us
    dot_general x1, matrix products, expert_apply(): jnp.einsum('sekd,edf->sekf', arrived, exp_up, preferred_element_type=jnp....  11.2 us
    gather x2, local copies, waits for them, and re-layouts, body(): jnp.take(returned, jnp.minimum(slot_index, device_count * slot_block - 1)...  10.5 us
  transfers between devices with their start and end apart: 7, of which 4 were waited for; matrix products, arithmetic and copies ran while one was open for 33% of the time, Pallas kernels for 0%

commit v1 on v0

v1 whole, which is shorter than its diff:
```python
import functools

import jax
import jax.numpy as jnp
from jax import lax
from jax.experimental import pallas as pl
from jax.experimental.pallas import tpu as pltpu
from jax.sharding import PartitionSpec as P

EPSILON = 1e-06
MESH = pl.DeviceIdType.MESH
BF = jnp.bfloat16
F32 = jnp.float32
NT = (((1,), (1,)), ((), ()))
TN = (((0,), (0,)), ((), ()))

Z_AG, Z_RET, Z_HELD, CODE_A, CODE_B, CR_Z, CR_X, CR_Y, CR_K = 0, 6, 9, 12, 15, 18, 21, 24, 27
PROB_A, PROB_B, X_AG, Y_AG, S_AG, DIS_A, DIS_B, S_RS = 28, 31, 34, 40, 46, 52, 60, 68
RET_A, RET_B, SUM_A, SUM_B, COPIES = 71, 79, 87, 90, 93


def dot(a, b):
    return jnp.dot(a, b, preferred_element_type=F32)


def iota(shape, dim):
    return lax.broadcasted_iota(jnp.int32, shape, dim)


def kernel(
    pre, held, source, resid, live, ids, pick, w_out_h, gain, router_t, wg_h, wu_h, wd_h, sg_h, su_h, sd_h,
    out, copy_rows,
    w_out, wg, wu, wd, sg, su, sd,
    hid, zb, pb, pr, hps, hr, idsp, code_a, code_b, ca, cb, svt, crz, crx, cry, crk, crs,
    prob_a, prob_b, pa, pb_b, buf_a, buf_b, sb, sp, sr, onehot, s2a, s2b, r2a, r2b, inner_a, inner_b,
    r3a, r3b, wca, wcb, s4a, s4b, r4a, r4b,
    ss, rs, ws, ls,
):
    a = lax.axis_index("dp")
    c = lax.axis_index("expert")
    x, y, k = c // 8, lax.rem(c // 2, 4), lax.rem(c, 2)

    def at(z_, x_, y_, k_):
        return (z_, (x_ * 4 + y_) * 2 + k_)

    def m4(v):
        return lax.rem(v, 4)

    loads = [
        pltpu.make_async_copy(src, dst, ws.at[i])
        for i, (src, dst) in enumerate(
            [(w_out_h, w_out), (sg_h, sg), (su_h, su), (sd_h, sd), (wg_h.at[0], wg), (wu_h.at[0], wu), (wd_h.at[0], wd)]
        )
    ]
    for load in loads:
        load.start()

    sent, finished = [], set()

    def send(i, src, dst, device):
        copy = pltpu.make_async_remote_copy(
            src_ref=src, dst_ref=dst, send_sem=ss.at[i], recv_sem=rs.at[i], device_id=device, device_id_type=MESH
        )
        copy.start()
        sent.append(copy)
        return copy

    zdev = lambda i: at(i, x, y, k)
    xdev = lambda i: at(a, i, y, k)
    ydev = lambda i: at(a, x, i, k)

    def others(me, base, dev, src, dst):
        return [send(base + i - 1, src(m4(me + i)), dst(m4(me + i)), dev(m4(me + i))) for i in (1, 2, 3)]

    def ring(base, buf, me, dev):
        right, left = m4(me + 1), m4(me + 3)
        top, bottom = pl.ds(0, 64), pl.ds(64, 64)
        go = lambda i, slot, part, to: send(base + i, buf.at[slot, part], buf.at[slot, part], dev(to))
        copies = [go(0, me, top, right), go(1, me, bottom, left), go(2, me, bottom, right), go(3, me, top, left)]

        def forward():
            copies[0].wait_recv()
            copies.append(go(4, left, top, right))
            copies[1].wait_recv()
            copies.append(go(5, right, bottom, left))

        return copies, forward

    hid[0:120, :] = pre[...].astype(F32)
    hid[120:128, :] = jnp.zeros((8, 2048), F32)
    hid[120:124, :] = held[...].astype(F32)
    zb[a] = hid[...].astype(BF)

    barrier = pltpu.get_barrier_semaphore()
    peers = [at(m4(a + i), x, y, k) for i in (1, 2, 3)]
    peers += [at(a, x, m4(y + i), lax.rem(k + j, 2)) for i in range(4) for j in range(2) if i or j]
    peers += [at(a, m4(x + i), y, lax.rem(k + j, 2)) for i in (1, 2, 3) for j in range(2)]
    for peer in peers:
        pl.semaphore_signal(barrier, inc=1, device_id=peer, device_id_type=MESH)
    pl.semaphore_wait(barrier, len(peers))

    z_copies, z_forward = ring(Z_AG, zb, a, zdev)

    idsp[...] = jnp.full((8, 128), -1, jnp.int32)
    idsp[0:6, 0:124] = ids[...]
    lane = iota((32, 128), 1)
    row = iota((32, 128), 0)
    alive = (lane < live[0]) | (lane >= 120)
    before = jnp.where(iota((128, 128), 0) < iota((128, 128), 1), 1.0, 0.0).astype(BF)

    def match(expert):
        hit = idsp[0:1, :] == expert
        for i in range(1, 6):
            hit = hit | (idsp[i : i + 1, :] == expert)
        return jnp.where(hit & alive, 1.0, 0.0)

    hits = match(row)
    ranks = dot(hits.astype(BF), before)
    code_a[...] = jnp.where(hits > 0.5, ranks + (24 * x).astype(F32), -1.0)
    hits_b = match(lax.rem(row // 2, 4) * 8 + row // 8 * 2 + lax.rem(row, 2))
    ranks_b = dot(hits_b.astype(BF), before)
    code_b[...] = jnp.where(hits_b > 0.5, ranks_b + (24 * y).astype(F32), -1.0)

    def tile(ref, i):
        return ref.at[pl.ds(pl.multiple_of(i * 8, 8), 8)]

    ca[x] = code_a[pl.ds(pl.multiple_of(x * 8, 8), 8), :]
    cb[y] = code_b[pl.ds(pl.multiple_of(y * 8, 8), 8), :]
    code_copies = others(x, CODE_A, xdev, lambda i: tile(code_a, i), lambda i: ca.at[x])
    code_copies += others(y, CODE_B, ydev, lambda i: tile(code_b, i), lambda i: cb.at[y])

    counts = lax.dot_general(jnp.ones((8, 128), BF), hits.astype(BF), NT, preferred_element_type=F32)
    copy_index = iota((8, 32), 0)
    offset = lax.rem(copy_index - pick[...] + 4, 4)
    served = (counts.astype(jnp.int32) - offset + 3) // 4
    svt[...] = jnp.zeros((8, 128), F32)
    svt[:, 0:32] = jnp.where(copy_index < 4, served, 0).astype(F32)
    crz[a] = svt[...]
    cr_copies = others(a, CR_Z, zdev, lambda i: svt, lambda i: crz.at[a])

    loads[0].wait()

    def project(slot):
        pb[slot] = dot(zb[slot], w_out[...]).astype(BF)

    project(a)
    pr[a] = pb[a]
    left, right, opposite = m4(a + 3), m4(a + 1), m4(a + 2)
    z_forward()
    returns = []
    for i, (slot, parts) in enumerate(((left, (2,)), (right, (3,)), (opposite, (4, 5)))):
        for part in parts:
            z_copies[part].wait_recv()
        project(slot)
        returns.append(send(Z_RET + i, pb.at[slot], pr.at[a], zdev(slot)))
    place_row, place_col = iota((16, 512), 0), iota((16, 512), 1)
    place_t = lax.rem(place_col, 128)
    place = (place_t >= 120) & (place_t < 124) & (place_row == place_col // 128 * 4 + place_t - 120)
    hps[...] = dot(jnp.where(place, 1.0, 0.0).astype(BF), pb[...].reshape(512, 512)).astype(BF)
    hr[a] = hps[...]
    returns += others(a, Z_HELD, zdev, lambda i: hps, lambda i: hr.at[a])

    for copy in cr_copies:
        copy.wait_recv()
    crs[0] = crz[0] + crz[1] + crz[2] + crz[3]
    crx[x] = crs[0]
    cr_copies = others(x, CR_X, xdev, lambda i: crs.at[0], lambda i: crx.at[x])

    hid[120:128, :] = jnp.zeros((8, 2048), F32)
    hid[0:124, :] = resid[...].astype(F32)
    sel_t, sel_i = iota((128, 16), 0), iota((128, 16), 1)
    chosen = jnp.full((128, 16), -1, jnp.int32)
    for i in range(4):
        chosen = jnp.where(sel_t == 120 + i, source[i], chosen)
    select = jnp.where(sel_i == chosen, 1.0, 0.0).astype(BF)
    prefill = iota((128, 512), 0) < 120
    for copy in returns:
        copy.wait_recv()
    for i in range(4):
        cols = slice(i * 512, i * 512 + 512)
        hid[:, cols] = hid[:, cols] + jnp.where(prefill, pr[i].astype(F32), dot(select, hr[i]))

    def norm(i, _):
        rows = pl.ds(pl.multiple_of(i * 16, 16), 16)
        v = hid[rows, :]
        scale = lax.rsqrt(jnp.mean(v * v, axis=1, keepdims=True) + EPSILON)
        normed = (v * scale * gain[...]).astype(BF)
        buf_a[x, rows, :] = normed[:, 0:1024]
        buf_b[y, rows, :] = normed[:, 1024:2048]
        sb[a, rows, :] = normed
        return 0

    lax.fori_loop(0, 8, norm, 0)
    x_copies, x_forward = ring(X_AG, buf_a, x, xdev)
    y_copies, y_forward = ring(Y_AG, buf_b, y, ydev)
    s_copies, s_forward = ring(S_AG, sb, a, zdev)

    logits = lax.dot_general(router_t[...], sb[a], NT, preferred_element_type=F32)
    powers = jnp.exp(logits - jnp.max(logits, axis=0, keepdims=True))
    prob_a[...] = powers / jnp.sum(powers, axis=0, keepdims=True)
    for i in range(16):
        j = i % 4 * 4 + i // 4
        prob_b[2 * i : 2 * i + 2, :] = prob_a[2 * j : 2 * j + 2, :]
    pa[x] = prob_a[pl.ds(pl.multiple_of(x * 8, 8), 8), :]
    pb_b[y] = prob_b[pl.ds(pl.multiple_of(y * 8, 8), 8), :]
    prob_copies = others(x, PROB_A, xdev, lambda i: tile(prob_a, i), lambda i: pa.at[x])
    prob_copies += others(y, PROB_B, ydev, lambda i: tile(prob_b, i), lambda i: pb_b.at[y])

    x_forward()
    y_forward()
    for copy in cr_copies:
        copy.wait_recv()
    crs[1] = crx[0] + crx[1] + crx[2] + crx[3]
    cry[y] = crs[1]
    cr_copies = others(y, CR_Y, ydev, lambda i: crs.at[1], lambda i: cry.at[y])
    for copy in code_copies:
        copy.wait_recv()

    slot96 = iota((96, 512), 0).astype(F32)

    def codes(ref, i):
        return jnp.concatenate([ref[s, pl.ds(i, 1), :] for s in range(4)], axis=1)

    locals_ = []

    def dispatch(base, step, core, code, buf, slots, landing, me, dev, group):
        for i in range(4):
            onehot[96 * i : 96 * i + 96, :] = jnp.where(slot96 == codes(code, 2 * i + core), 1.0, 0.0).astype(BF)

        def columns(n, _):
            cols = pl.ds(pl.multiple_of(n * 256, 256), 256)
            rows = buf[:, :, cols].reshape(512, 256)
            slots[core, :, :, cols] = dot(onehot[...], rows).astype(BF).reshape(4, 96, 256)
            return 0

        lax.fori_loop(0, 4, columns, 0)
        copies = []
        for i in range(4):
            to = m4(me + i)
            if step == 0 and i == 0:
                copy = pltpu.make_async_copy(slots.at[core, to], landing.at[k, me], ls.at[base])
                copy.start()
                locals_.append(copy)
                continue
            copies.append(send(group + 4 * step + i, slots.at[core, to], landing.at[k, me], dev(to, core)))
        return copies

    col_dev = lambda i, core: at(a, x, i, core)
    row_dev = lambda i, core: at(a, i, y, core)
    for copy in x_copies[2:]:
        copy.wait_recv()
    arrive = [[], []]
    arrive[0] += dispatch(0, 0, k, ca, buf_a, s2a, r2a, y, col_dev, DIS_A)
    for copy in y_copies[2:]:
        copy.wait_recv()
    arrive[0] += dispatch(1, 0, k, cb, buf_b, s2b, r2b, x, row_dev, DIS_B)
    arrive[1] += dispatch(0, 1, 1 - k, ca, buf_a, s2a, r2a, y, col_dev, DIS_A)
    arrive[1] += dispatch(1, 1, 1 - k, cb, buf_b, s2b, r2b, x, row_dev, DIS_B)

    s_forward()
    for copy in s_copies[2:]:
        copy.wait_recv()
    for load in loads[1:4]:
        load.wait()

    def shared(i, _):
        rows = sb[i]
        gate = lax.dot_general(rows, sg[...], NT, preferred_element_type=F32)
        up = lax.dot_general(rows, su[...], NT, preferred_element_type=F32)
        hidden_units = (gate / (1.0 + jnp.exp(-gate)) * up).astype(BF)

        def columns(n, _):
            cols = pl.ds(pl.multiple_of(n * 512, 512), 512)
            sp[i, :, cols] = dot(hidden_units, sd[:, cols]).astype(BF)
            return 0

        lax.fori_loop(0, 4, columns, 0)
        return 0

    lax.fori_loop(0, 4, shared, 0)
    shared_copies = others(a, S_RS, zdev, lambda i: sp.at[i], lambda i: sr.at[a])
    sr[a] = sp[a]

    for copy in prob_copies:
        copy.wait_recv()

    def weights(code, prob, into):
        for i in range(8):
            e = lax.rem(i, 4) * 2 + i // 4
            hit = slot96 == codes(code, e)
            into[96 * i : 96 * i + 96, :] = jnp.where(hit, codes(prob, e), 0.0).astype(BF)

    weights(ca, pa, wca)
    weights(cb, pb_b, wcb)

    for copy in cr_copies:
        copy.wait_recv()
    crs[2] = cry[0] + cry[1] + cry[2] + cry[3]
    crk[k] = crs[2]
    cr_copy = send(CR_K, crs.at[2], crk.at[k], at(a, x, y, 1 - k))

    for load in loads[4:]:
        load.wait()

    def swapped(v):
        return jnp.concatenate([v[(j * 4 + i) * 24 : (j * 4 + i) * 24 + 24] for i in range(4) for j in range(4)], axis=0)

    def expert(step, core):
        for copy in arrive[step]:
            copy.wait_recv()
        if step == 0:
            for copy in locals_:
                copy.wait()

        def up(n, _):
            cols = pl.ds(pl.multiple_of(n * 128, 128), 128)
            first = jnp.concatenate([wg[0:1024, cols], wu[0:1024, cols]], axis=1)
            second = jnp.concatenate([wg[1024:2048, cols], wu[1024:2048, cols]], axis=1)
            h = dot(r2a[core].reshape(384, 1024), first) + swapped(dot(r2b[core].reshape(384, 1024), second))
            gate = h[:, 0:128]
            inner = gate / (1.0 + jnp.exp(-gate)) * h[:, 128:256]
            inner_a[:, cols] = inner.astype(BF)
            inner_b[:, cols] = swapped(inner).astype(BF)
            return 0

        lax.fori_loop(0, 11, up, 0)
        for copy in arrive[step]:
            copy.wait_send()
            finished.add(id(copy))
        copies = []
        for group, inner, slots, landing, me, dev, first in (
            (RET_A, inner_a, s2a, r3a, y, col_dev, 0),
            (RET_B, inner_b, s2b, r3b, x, row_dev, 1024),
        ):

            def down(n, _):
                cols = pl.ds(pl.multiple_of(n * 256, 256), 256)
                wide = pl.ds(pl.multiple_of(first + n * 256, 256), 256)
                slots[core, :, :, cols] = dot(inner[...], wd[:, wide]).astype(BF).reshape(4, 96, 256)
                return 0

            lax.fori_loop(0, 4, down, 0)
            for i in range(4):
                to = m4(me + i)
                if step == 0 and i == 0:
                    copy = pltpu.make_async_copy(slots.at[core, to], landing.at[k, me], ls.at[2 + (group == RET_B)])
                    copy.start()
                    locals_.append(copy)
                    continue
                copies.append(send(group + 4 * step + i, slots.at[core, to], landing.at[k, me], dev(to, core)))
        return copies

    back = expert(0, k)
    back += expert(1, 1 - k)
    back_a, back_b = [back[i] for i in (0, 1, 2, 6, 7, 8, 9)], [back[i] for i in (3, 4, 5, 10, 11, 12, 13)]

    def combine(copies, local, wc, landed, sums, finals, me, dev, group):
        for copy in copies:
            copy.wait_recv()
        local.wait()

        def columns(n, _):
            cols = pl.ds(pl.multiple_of(n * 256, 256), 256)
            v = lax.dot_general(wc[...], landed[:, :, :, cols].reshape(768, 256), TN, preferred_element_type=F32)
            sums[:, :, cols] = v.astype(BF).reshape(4, 128, 256)
            return 0

        lax.fori_loop(0, 4, columns, 0)
        finals[me] = sums[me]
        return others(me, group, dev, lambda i: sums.at[i], lambda i: finals.at[me])

    last = combine(back_a, locals_[2], wca, r3a, s4a, r4a, x, xdev, SUM_A)
    last += combine(back_b, locals_[3], wcb, r3b, s4b, r4b, y, ydev, SUM_B)

    cr_copy.wait_recv()
    served_all = crk[0] + crk[1]
    mine = (iota((8, 128), 0) == a) & (iota((8, 128), 1) == c)
    copy_rows[0] = jnp.sum(jnp.where(mine, served_all, 0.0)).astype(jnp.int32)

    for copy in shared_copies + last:
        copy.wait_recv()
    for finals, first in ((r4a, 0), (r4b, 1024)):

        def total(n, _):
            cols = pl.ds(pl.multiple_of(n * 256, 256), 256)
            wide = pl.ds(pl.multiple_of(first + n * 256, 256), 256)
            v = hid[:, wide]
            for i in range(4):
                v = v + sr[i, :, wide].astype(F32)
            for i in range(4):
                v = v + finals[i, :, cols].astype(F32)
            out[:, wide] = v[0:124].astype(BF)
            return 0

        lax.fori_loop(0, 4, total, 0)
    for copy in sent:
        if id(copy) not in finished:
            copy.wait_send()


def body(
    attn_prefill, decode_held, decode_source, residual, live_rows, expert_ids, replica_pick, w_out, norm_gain, router,
    exp_gate, exp_up, exp_down, shared_gate, shared_up, shared_down,
):
    vmem = pl.BlockSpec(memory_space=pltpu.VMEM)
    smem = pl.BlockSpec(memory_space=pltpu.SMEM)
    hbm = pl.BlockSpec(memory_space=pl.ANY)
    V = pltpu.VMEM
    return pl.pallas_call(
        kernel,
        out_shape=(jax.ShapeDtypeStruct((124, 2048), BF), jax.ShapeDtypeStruct((1,), jnp.int32)),
        in_specs=[vmem, vmem, smem, vmem, smem, vmem, vmem, hbm, vmem, vmem, hbm, hbm, hbm, hbm, hbm, hbm],
        out_specs=(vmem, smem),
        scratch_shapes=[
            V((2048, 512), BF), V((2048, 1408), BF), V((2048, 1408), BF), V((1408, 2048), BF),
            V((352, 2048), BF), V((352, 2048), BF), V((352, 2048), BF),
            V((128, 2048), F32), V((4, 128, 2048), BF), V((4, 128, 512), BF), V((4, 128, 512), BF),
            V((16, 512), BF), V((4, 16, 512), BF),
            V((8, 128), jnp.int32), V((32, 128), F32), V((32, 128), F32), V((4, 8, 128), F32), V((4, 8, 128), F32),
            V((8, 128), F32), V((4, 8, 128), F32), V((4, 8, 128), F32), V((4, 8, 128), F32), V((2, 8, 128), F32),
            V((3, 8, 128), F32),
            V((32, 128), F32), V((32, 128), F32), V((4, 8, 128), F32), V((4, 8, 128), F32),
            V((4, 128, 1024), BF), V((4, 128, 1024), BF),
            V((4, 128, 2048), BF), V((4, 128, 2048), BF), V((4, 128, 2048), BF),
            V((384, 512), BF),
            V((2, 4, 96, 1024), BF), V((2, 4, 96, 1024), BF), V((2, 4, 96, 1024), BF), V((2, 4, 96, 1024), BF),
            V((384, 1408), BF), V((384, 1408), BF),
            V((2, 4, 96, 1024), BF), V((2, 4, 96, 1024), BF),
            V((768, 512), BF), V((768, 512), BF),
            V((4, 128, 1024), BF), V((4, 128, 1024), BF), V((4, 128, 1024), BF), V((4, 128, 1024), BF),
            pltpu.SemaphoreType.DMA((COPIES,)), pltpu.SemaphoreType.DMA((COPIES,)),
            pltpu.SemaphoreType.DMA((7,)), pltpu.SemaphoreType.DMA((4,)),
        ],
        compiler_params=pltpu.CompilerParams(collective_id=0, has_side_effects=True, vmem_limit_bytes=62 << 20),
        cost_estimate=pl.CostEstimate(flops=17_000_000_000, bytes_accessed=26_000_000, transcendentals=2_000_000),
        name="moe",
    )(
        attn_prefill, decode_held, decode_source, residual, live_rows, expert_ids.T, replica_pick, w_out,
        norm_gain.reshape(1, 2048), router.T, exp_gate, exp_up, exp_down, shared_gate, shared_up, shared_down,
    )


def solution(mesh):
    rows = P(("dp", "expert"), None)
    flat = P(("dp", "expert"))
    placed = (
        rows, rows, flat, rows, flat, rows, rows, P(None, "dp"), P(), P(),
        P("expert", None, None), P("expert", None, None), P("expert", None, None),
        P("dp", None), P("dp", None), P("dp", None),
    )
    return jax.shard_map(body, mesh=mesh, in_specs=placed, out_specs=(rows, flat), check_vma=False)
```

time: 337 us -> 122 us (0.36)
  Pallas kernels: 0 us -> 117 us
  waiting for transfers between devices: 98 us -> 0 us
  blocking collectives: 74.5 us -> 0 us
  local copies, waits for them, and re-layouts: 60.4 us -> 1.88 us
  matrix products: 41 us -> 0 us
  starting transfers between devices: 31.6 us -> 0 us
  other arithmetic: 14.1 us -> 0 us
  between operations: 15.8 us -> 2.99 us
    pallas_call x0 -> x1, Pallas kernels: none -> 117 us  [body(): pl.pallas_call(kernel, out_shape=(jax.ShapeDtypeStruct((124, 2048), BF),...]
    all_gather x2 -> x0, waiting for transfers between devices: 92.4 us -> none  [the longest x1 61.7 us: body(): row_piece = lax.all_gather(normed, 'dp', axis=0, tiled=True)]
    unnamed x1 -> x0, blocking collectives: 63 us -> none
    dot_general x6 -> x0, matrix products: 41 us -> none  [the longest x1 18.9 us: expert_apply(): jnp.einsum('sekf,efd->sekd', expert_inner, exp_down, preferred_element_ty...]
    all_to_all x4 -> x0, starting transfers between devices: 30.2 us -> none  [the longest x1 10.2 us: body(): lax.all_to_all(outgoing, ('dp', 'expert'), split_axis=0, concat_axis=0, t...]
    reshape x6 -> x0, local copies, waits for them, and re-layouts: 14.8 us -> none  [the longest x1 6.13 us: body(): source_rows = jnp.repeat(normed, top_count, axis=0)]
    scatter x2 -> x0, local copies, waits for them, and re-layouts: 12.9 us -> none  [the longest x1 8.84 us: body(): outgoing = jnp.zeros((device_count * slot_block, feature_width), jnp.bflo...]
    all_gather x1 -> x0, blocking collectives: 11.5 us -> none  [body(): group_rows = lax.all_gather(decode_held, 'dp', axis=0, tiled=True)]
  transfers between devices with their start and end apart: 7 -> 0, of which waited for: 4 -> 0; matrix products, arithmetic and copies ran while one was open for 33% -> 0% of each run, Pallas kernels for 0% -> 0%
where the time goes in v1:
time: 122 us
  Pallas kernels  117 us (96%)
  between operations  2.99 us (2%)
  local copies, waits for them, and re-layouts  1.88 us (2%)
    pallas_call x1, Pallas kernels, body(): pl.pallas_call(kernel, out_shape=(jax.ShapeDtypeStruct((124, 2048), BF),...  117 us

profile of v1, /device:TPU:1, one launch (start us, length us, event | category | flops | bytes accessed | tf_op | source)
XLA Modules:
  0.0 121.6 jit_solution(9576250610742624932)
XLA Ops:
  1.3 116.7 %moe.1 = (bf16[124,2048]{1,0:T(8,128)(2,1)}, s32[1]{0:T(128)}) custom-call(bf16[120,2048]{1,0:T(8,128)(2,1)} %pre.1, bf16[4,2048]{1,0:T(4,128)(2,1)} %held.1, s32[4]{0:T(128)} %source.1, bf16[124,2048]{1,0:T(8,128)(2,1)} %resid.1, s32[1]{0:T(128)S(6)} %copy.20.live, s32[6,124]{1,0:T(8,128)} %bitcast.5, s32[1,32]{1,0:T(1,128)} %pick.1, ...), custom_call_target="tpu_custom_call" | custom-call | flops 16999999488 | bytes 26000000 | tf_op jit(solution)/shard_map/moe/pallas_call | solution.py:409
  118.0 1.9 %copy.21 = bf16[124,2048]{1,0:T(8,128)(2,1)} copy(bf16[124,2048]{1,0:T(8,128)(2,1)} %get-tuple-element.4) | data formatting | bytes 1015808

commit v2 on v1

v2 whole, which is shorter than its diff:
```python
import functools

import jax
import jax.numpy as jnp
from jax import lax
from jax.experimental import pallas as pl
from jax.experimental.pallas import tpu as pltpu
from jax.sharding import PartitionSpec as P

EPSILON = 1e-06
MESH = pl.DeviceIdType.MESH
BF = jnp.bfloat16
F32 = jnp.float32
NT = (((1,), (1,)), ((), ()))

GROUPS = dict(
    Z_TOP=2, Z_BOTTOM=2, Z_RET=2, HELD=3, W_PIECE=2, WA_X=6, WA_Y=6, WB_Y=6, WB_X=6, W_CORE=2, CODE_A=3, CODE_B=3, CR_Z=3,
    CR_X=3, CR_Y=3, CR_K=1, PROB_A=3, PROB_B=3, X_AG=6, Y_AG=6, S_AG=6, DIS_A=8, DIS_B=8, S_SUM=6, RET_A=8, RET_B=8, SUM_A=6, SUM_B=6,
)
COPIES = sum(GROUPS.values())
ID = {name: sum(list(GROUPS.values())[:i]) for i, name in enumerate(GROUPS)}


def dot(a, b):
    return jnp.dot(a, b, preferred_element_type=F32)


def iota(shape, dim):
    return lax.broadcasted_iota(jnp.int32, shape, dim)


def kernel(
    pre, held, source, resid, live, ids, pick, w_out_h, gain, router_t, wg_h, wu_h, wd_h, sg_h, su_h, sd_h,
    out, copy_rows,
    w_out, wg, wu, wd, sg, su, sd,
    hid, zb, pb, pr, held_f, held_s, held_all, wo_a, wo_b, idsp, code_a, code_b, ca, cb, svt, crz, crx, cry, crk, crs,
    prob_a, prob_b, pa, pb_b, buf_a, buf_b, sb, sp, s_mid, sr, onehot, s2a, s2b, r2a, r2b, inner_a, inner_b,
    r3a, r3b, wide, wca, wcb, s4a, s4b, mid_a, mid_b, r4a, r4b,
    ss, rs, ws, ls,
):
    a = lax.axis_index("dp")
    c = lax.axis_index("expert")
    x, y, k = c // 8, lax.rem(c // 2, 4), lax.rem(c, 2)

    def at(z_, x_, y_, k_):
        return (z_, (x_ * 4 + y_) * 2 + k_)

    def m4(v):
        return lax.rem(v, 4)

    loads = [
        pltpu.make_async_copy(src, dst, ws.at[i])
        for i, (src, dst) in enumerate(
            [(w_out_h, w_out), (sg_h, sg), (su_h, su), (sd_h, sd), (wg_h.at[0], wg), (wu_h.at[0], wu), (wd_h.at[0], wd)]
        )
    ]
    loads[0].start()

    barrier = pltpu.get_barrier_semaphore()
    peers = [at(m4(a + i), x, y, k) for i in (1, 2, 3)]
    peers += [at(a, x, m4(y + i), lax.rem(k + j, 2)) for i in range(4) for j in range(2) if i or j]
    peers += [at(a, m4(x + i), y, lax.rem(k + j, 2)) for i in (1, 2, 3) for j in range(2)]
    for peer in peers:
        pl.semaphore_signal(barrier, inc=1, device_id=peer, device_id_type=MESH)

    sent, finished = [], set()

    def send(i, src, dst, device):
        copy = pltpu.make_async_remote_copy(
            src_ref=src, dst_ref=dst, send_sem=ss.at[i], recv_sem=rs.at[i], device_id=device, device_id_type=MESH
        )
        copy.start()
        sent.append(copy)
        return copy

    zdev = lambda i: at(i, x, y, k)
    xdev = lambda i: at(a, i, y, k)
    ydev = lambda i: at(a, x, i, k)

    def others(me, base, dev, src, dst):
        return [send(base + i - 1, src(m4(me + i)), dst(m4(me + i)), dev(m4(me + i))) for i in (1, 2, 3)]

    def ring(base, buf, me, dev, half=64):
        right, left = m4(me + 1), m4(me + 3)
        top, bottom = pl.ds(0, half), pl.ds(half, half)
        go = lambda i, slot, part, to: send(base + i, buf.at[slot, part], buf.at[slot, part], dev(to))
        copies = [go(0, me, top, right), go(1, me, bottom, left), go(2, me, bottom, right), go(3, me, top, left)]

        def forward():
            copies[0].wait_recv()
            copies.append(go(4, left, top, right))
            copies[1].wait_recv()
            copies.append(go(5, right, bottom, left))

        return copies, forward

    def ring_sum(base, sums, middle, finals, me, dev):
        right, left, far = m4(me + 1), m4(me + 3), m4(me + 2)
        top, bottom = pl.ds(0, 64), pl.ds(64, 64)
        copies = {}

        def go(i, slot, part, landing, to):
            copies[i] = send(base + i, sums.at[slot, part], landing, dev(to))

        def far_ready():
            go(0, far, top, middle.at[0], right)
            go(1, far, bottom, middle.at[1], left)

        def right_ready():
            go(2, right, bottom, finals.at[0, bottom], right)

        def left_ready():
            go(3, left, top, finals.at[1, top], left)

        def pass_on():
            copies[0].wait_recv()
            sums[right, top, :] = (sums[right, top, :].astype(F32) + middle[0].astype(F32)).astype(BF)
            go(4, right, top, finals.at[0, top], right)
            copies[1].wait_recv()
            sums[left, bottom, :] = (sums[left, bottom, :].astype(F32) + middle[1].astype(F32)).astype(BF)
            go(5, left, bottom, finals.at[1, bottom], left)

        def landed():
            for i in (2, 3, 4, 5):
                copies[i].wait_recv()

        return far_ready, right_ready, left_ready, pass_on, landed

    left, right, opposite = m4(a + 3), m4(a + 1), m4(a + 2)
    top, bottom = pl.ds(0, 64), pl.ds(64, 64)
    hid[0:120, :] = pre[...].astype(F32)
    hid[120:128, :] = jnp.zeros((8, 2048), F32)
    zb[0, 0:64, :] = hid[0:64, :].astype(BF)
    for i in range(4):
        held_f[4 * i : 4 * i + 4, :] = held[:, 512 * i : 512 * i + 512].astype(F32)
    held_s[...] = held_f[...].astype(BF)
    held_all[a] = held_s[...]
    loads[0].wait()

    pl.semaphore_wait(barrier, len(peers))

    piece_rows = pl.ds(pl.multiple_of((x * 4 + y) * 128, 128), 128)
    piece_cols = lambda i: pl.ds(pl.multiple_of(k * 256 + i * 128, 128), 128)
    pieces = [send(ID["W_PIECE"], w_out.at[piece_rows, piece_cols(0)], wo_a.at[k, y, x], zdev(opposite))]
    pieces += [send(ID["W_PIECE"] + 1, w_out.at[piece_rows, piece_cols(1)], wo_b.at[k, x, y], zdev(opposite))]
    held_copies = others(a, ID["HELD"], zdev, lambda i: held_s, lambda i: held_all.at[a])

    def both(base, part):
        return [
            send(base, zb.at[0, part], zb.at[1, part], zdev(right)),
            send(base + 1, zb.at[0, part], zb.at[2, part], zdev(left)),
        ]

    tops = both(ID["Z_TOP"], top)
    for load in loads[1:]:
        load.start()

    idsp[...] = jnp.full((8, 128), -1, jnp.int32)
    idsp[0:6, 0:124] = ids[...]
    lane = iota((32, 128), 1)
    row = iota((32, 128), 0)
    alive = (lane < live[0]) | (lane >= 120)
    before = jnp.where(iota((128, 128), 0) < iota((128, 128), 1), 1.0, 0.0).astype(BF)

    def match(expert):
        hit = idsp[0:1, :] == expert
        for i in range(1, 6):
            hit = hit | (idsp[i : i + 1, :] == expert)
        return jnp.where(hit & alive, 1.0, 0.0)

    hits = match(row)
    ranks = dot(hits.astype(BF), before)
    code_a[...] = jnp.where(hits > 0.5, ranks + (24 * x).astype(F32), -1.0)
    hits_b = match(lax.rem(row // 2, 4) * 8 + row // 8 * 2 + lax.rem(row, 2))
    ranks_b = dot(hits_b.astype(BF), before)
    code_b[...] = jnp.where(hits_b > 0.5, ranks_b + (24 * y).astype(F32), -1.0)

    def tile(ref, i):
        return ref.at[pl.ds(pl.multiple_of(i * 8, 8), 8)]

    ca[x] = code_a[pl.ds(pl.multiple_of(x * 8, 8), 8), :]
    cb[y] = code_b[pl.ds(pl.multiple_of(y * 8, 8), 8), :]
    code_copies = others(x, ID["CODE_A"], xdev, lambda i: tile(code_a, i), lambda i: ca.at[x])
    code_copies += others(y, ID["CODE_B"], ydev, lambda i: tile(code_b, i), lambda i: cb.at[y])

    counts = lax.dot_general(jnp.ones((8, 128), BF), hits.astype(BF), NT, preferred_element_type=F32)
    copy_index = iota((8, 32), 0)
    offset = lax.rem(copy_index - pick[...] + 4, 4)
    served = (counts.astype(jnp.int32) - offset + 3) // 4
    svt[...] = jnp.zeros((8, 128), F32)
    svt[:, 0:32] = jnp.where(copy_index < 4, served, 0).astype(F32)
    crz[a] = svt[...]
    cr_copies = others(a, ID["CR_Z"], zdev, lambda i: svt, lambda i: crz.at[a])

    row64, col64 = iota((64, 64), 0), iota((64, 64), 1)
    chosen = jnp.full((64, 64), -64, jnp.int32)
    for i in range(4):
        chosen = jnp.where(row64 == 56 + i, source[i] // 4 * 16 + lax.rem(source[i], 4), chosen)
    for copy in held_copies:
        copy.wait_recv()
    for i in range(4):
        cols = slice(512 * i, 512 * i + 512)
        picked = dot(jnp.where(col64 == chosen + 4 * i, 1.0, 0.0).astype(BF), held_all[...].reshape(64, 512))
        zb[0, 64:128, cols] = (hid[64:128, cols] + picked).astype(BF)
    bottoms = both(ID["Z_BOTTOM"], bottom)
    for copy in pieces:
        copy.wait_recv()
    ax_copies, ax_forward = ring(ID["WA_X"], wo_a.at[k, y], x, xdev)
    by_copies, by_forward = ring(ID["WB_Y"], wo_b.at[k, x], y, ydev)
    pr[a] = dot(zb[0], w_out[...]).astype(BF)
    ax_forward()
    by_forward()
    for copy in ax_copies[2:]:
        copy.wait_recv()
    ay_copies, ay_forward = ring(ID["WA_Y"], wo_a.at[k], y, ydev, 2)
    for copy in by_copies[2:]:
        copy.wait_recv()
    bx_copies, bx_forward = ring(ID["WB_X"], wo_b.at[k], x, xdev, 2)
    ay_forward()
    bx_forward()
    for copy in ay_copies[2:]:
        copy.wait_recv()
    core_copies = [send(ID["W_CORE"], wo_a.at[k], wo_a.at[k], at(a, x, y, 1 - k))]
    for copy in bx_copies[2:]:
        copy.wait_recv()
    core_copies += [send(ID["W_CORE"] + 1, wo_b.at[k], wo_b.at[k], at(a, x, y, 1 - k))]
    returns = []
    for i, slot in enumerate((left, right)):
        tops[i].wait_recv()
        bottoms[i].wait_recv()
        pb[i] = dot(zb[1 + i], w_out[...]).astype(BF)
        returns.append(send(ID["Z_RET"] + i, pb.at[i], pr.at[a], zdev(slot)))
    for copy in core_copies:
        copy.wait_recv()
    far = jnp.zeros((128, 512), F32)
    for i in range(8):
        rows = [
            jnp.concatenate([wo_a[0, n, m], wo_b[0, m, n], wo_a[1, n, m], wo_b[1, m, n]], axis=1)
            for m, n in ((i // 2, i % 2 * 2), (i // 2, i % 2 * 2 + 1))
        ]
        far = far + dot(zb[0, :, 256 * i : 256 * i + 256], jnp.concatenate(rows, axis=0))
    pr[opposite] = far.astype(BF)

    for copy in cr_copies:
        copy.wait_recv()
    crs[0] = crz[0] + crz[1] + crz[2] + crz[3]
    crx[x] = crs[0]
    cr_copies = others(x, ID["CR_X"], xdev, lambda i: crs.at[0], lambda i: crx.at[x])

    hid[120:128, :] = jnp.zeros((8, 2048), F32)
    hid[0:124, :] = resid[...].astype(F32)
    for copy in returns:
        copy.wait_recv()
    for i in range(4):
        cols = slice(i * 512, i * 512 + 512)
        hid[:, cols] = hid[:, cols] + pr[i].astype(F32)

    def norm(i, _):
        rows = pl.ds(pl.multiple_of(i * 16, 16), 16)
        v = hid[rows, :]
        scale = lax.rsqrt(jnp.mean(v * v, axis=1, keepdims=True) + EPSILON)
        normed = (v * scale * gain[...]).astype(BF)
        buf_a[x, rows, :] = normed[:, 0:1024]
        buf_b[y, rows, :] = normed[:, 1024:2048]
        sb[a, rows, :] = normed
        return 0

    lax.fori_loop(0, 8, norm, 0)
    x_copies, x_forward = ring(ID["X_AG"], buf_a, x, xdev)
    y_copies, y_forward = ring(ID["Y_AG"], buf_b, y, ydev)
    s_copies, s_forward = ring(ID["S_AG"], sb, a, zdev)

    logits = lax.dot_general(router_t[...], sb[a], NT, preferred_element_type=F32)
    powers = jnp.exp(logits - jnp.max(logits, axis=0, keepdims=True))
    prob_a[...] = powers / jnp.sum(powers, axis=0, keepdims=True)
    for i in range(16):
        j = i % 4 * 4 + i // 4
        prob_b[2 * i : 2 * i + 2, :] = prob_a[2 * j : 2 * j + 2, :]
    pa[x] = prob_a[pl.ds(pl.multiple_of(x * 8, 8), 8), :]
    pb_b[y] = prob_b[pl.ds(pl.multiple_of(y * 8, 8), 8), :]
    prob_copies = others(x, ID["PROB_A"], xdev, lambda i: tile(prob_a, i), lambda i: pa.at[x])
    prob_copies += others(y, ID["PROB_B"], ydev, lambda i: tile(prob_b, i), lambda i: pb_b.at[y])

    x_forward()
    y_forward()
    s_forward()
    for copy in cr_copies:
        copy.wait_recv()
    crs[1] = crx[0] + crx[1] + crx[2] + crx[3]
    cry[y] = crs[1]
    cr_copies = others(y, ID["CR_Y"], ydev, lambda i: crs.at[1], lambda i: cry.at[y])
    for copy in code_copies:
        copy.wait_recv()

    slot96 = iota((96, 512), 0).astype(F32)

    def codes(ref, i):
        return jnp.concatenate([ref[s, pl.ds(i, 1), :] for s in range(4)], axis=1)

    locals_ = []

    def dispatch(base, step, core, code, buf, slots, landing, me, dev, group):
        for i in range(4):
            onehot[96 * i : 96 * i + 96, :] = jnp.where(slot96 == codes(code, 2 * i + core), 1.0, 0.0).astype(BF)

        def columns(n, _):
            cols = pl.ds(pl.multiple_of(n * 256, 256), 256)
            rows = buf[:, :, cols].reshape(512, 256)
            slots[core, :, :, cols] = dot(onehot[...], rows).astype(BF).reshape(4, 96, 256)
            return 0

        lax.fori_loop(0, 4, columns, 0, unroll=True)
        copies = []
        for i in range(4):
            to = m4(me + i)
            if step == 0 and i == 0:
                copy = pltpu.make_async_copy(slots.at[core, to], landing.at[k, me], ls.at[base])
                copy.start()
                locals_.append(copy)
                continue
            copies.append(send(group + 4 * step + i, slots.at[core, to], landing.at[k, me], dev(to, core)))
        return copies

    col_dev = lambda i, core: at(a, x, i, core)
    row_dev = lambda i, core: at(a, i, y, core)
    for copy in x_copies[2:]:
        copy.wait_recv()
    arrive = [[], []]
    arrive[0] += dispatch(0, 0, k, ca, buf_a, s2a, r2a, y, col_dev, ID["DIS_A"])
    for copy in y_copies[2:]:
        copy.wait_recv()
    arrive[0] += dispatch(1, 0, k, cb, buf_b, s2b, r2b, x, row_dev, ID["DIS_B"])
    arrive[1] += dispatch(0, 1, 1 - k, ca, buf_a, s2a, r2a, y, col_dev, ID["DIS_A"])
    arrive[1] += dispatch(1, 1, 1 - k, cb, buf_b, s2b, r2b, x, row_dev, ID["DIS_B"])

    for load in loads[1:4]:
        load.wait()

    def shared(i):
        rows = sb[i]
        gate = lax.dot_general(rows, sg[...], NT, preferred_element_type=F32)
        up = lax.dot_general(rows, su[...], NT, preferred_element_type=F32)
        hidden_units = (gate / (1.0 + jnp.exp(-gate)) * up).astype(BF)

        def columns(n, _):
            cols = pl.ds(pl.multiple_of(n * 512, 512), 512)
            sp[i, :, cols] = dot(hidden_units, sd[:, cols]).astype(BF)
            return 0

        lax.fori_loop(0, 4, columns, 0, unroll=True)

    def shared_of(i, parts):
        for part in parts:
            s_copies[part].wait_recv()
        shared(m4(a + i))

    s_far, s_right, s_left, s_pass, s_landed = ring_sum(ID["S_SUM"], sp, s_mid, sr, a, zdev)
    shared(a)
    shared_of(3, (2,))
    s_left()
    shared_of(1, (3,))
    s_right()

    for copy in prob_copies:
        copy.wait_recv()

    def weights(code, prob, into):
        for i in range(8):
            e = lax.rem(i, 4) * 2 + i // 4
            hit = slot96 == codes(code, e)
            wide[96 * i : 96 * i + 96, :] = jnp.where(hit, codes(prob, e), 0.0)
        into[...] = wide[...].T.astype(BF)

    weights(ca, pa, wca)
    weights(cb, pb_b, wcb)

    for copy in cr_copies:
        copy.wait_recv()
    crs[2] = cry[0] + cry[1] + cry[2] + cry[3]
    crk[k] = crs[2]
    cr_copy = send(ID["CR_K"], crs.at[2], crk.at[k], at(a, x, y, 1 - k))

    for load in loads[4:]:
        load.wait()

    def swapped(v):
        return jnp.concatenate([v[(j * 4 + i) * 24 : (j * 4 + i) * 24 + 24] for i in range(4) for j in range(4)], axis=0)

    def expert(step, core):
        for copy in arrive[step]:
            copy.wait_recv()
        if step == 0:
            for copy in locals_:
                copy.wait()

        def up(cols):
            first = jnp.concatenate([wg[0:1024, cols], wu[0:1024, cols]], axis=1)
            second = jnp.concatenate([wg[1024:2048, cols], wu[1024:2048, cols]], axis=1)
            h = dot(r2a[core].reshape(384, 1024), first) + swapped(dot(r2b[core].reshape(384, 1024), second))
            width = h.shape[1] // 2
            gate = h[:, 0:width]
            inner = gate / (1.0 + jnp.exp(-gate)) * h[:, width : 2 * width]
            inner_a[:, cols] = inner.astype(BF)
            inner_b[:, cols] = swapped(inner).astype(BF)

        for first in range(0, 1408, 256):
            up(slice(first, min(first + 256, 1408)))
        for copy in arrive[step]:
            copy.wait_send()
            finished.add(id(copy))
        copies = []
        for group, inner, slots, landing, me, dev, first in (
            (ID["RET_A"], inner_a, s2a, r3a, y, col_dev, 0),
            (ID["RET_B"], inner_b, s2b, r3b, x, row_dev, 1024),
        ):

            for n in (0, 512):
                out_cols = dot(inner[...], wd[:, first + n : first + n + 512])
                slots[core, :, :, n : n + 512] = out_cols.astype(BF).reshape(4, 96, 512)
            for i in range(4):
                to = m4(me + i)
                if step == 0 and i == 0:
                    copy = pltpu.make_async_copy(slots.at[core, to], landing.at[k, me], ls.at[2 + (group == ID["RET_B"])])
                    copy.start()
                    locals_.append(copy)
                    continue
                copies.append(send(group + 4 * step + i, slots.at[core, to], landing.at[k, me], dev(to, core)))
        return copies

    back = expert(0, k)
    shared_of(2, (4, 5))
    s_far()
    back += expert(1, 1 - k)
    s_pass()
    back_a, back_b = [back[i] for i in (0, 1, 2, 6, 7, 8, 9)], [back[i] for i in (3, 4, 5, 10, 11, 12, 13)]

    def combine(wc, landed, sums, i):
        rows = pl.ds(pl.multiple_of(i * 128, 128), 128)
        sums[i] = dot(wc[rows, :], landed[...].reshape(768, 1024)).astype(BF)

    a_far, a_right, a_left, a_pass, a_landed = ring_sum(ID["SUM_A"], s4a, mid_a, r4a, x, xdev)
    b_far, b_right, b_left, b_pass, b_landed = ring_sum(ID["SUM_B"], s4b, mid_b, r4b, y, ydev)
    for copies, local, part, me, ready in ((back_a, locals_[2], (wca, r3a, s4a), x, a_far), (back_b, locals_[3], (wcb, r3b, s4b), y, b_far)):
        for copy in copies:
            copy.wait_recv()
        local.wait()
        combine(*part, m4(me + 2))
        ready()
    for part, me, rest in (((wca, r3a, s4a), x, (a_right, a_left)), ((wcb, r3b, s4b), y, (b_right, b_left))):
        combine(*part, m4(me + 1))
        rest[0]()
        combine(*part, m4(me + 3))
        rest[1]()
    a_pass()
    b_pass()
    combine(wca, r3a, s4a, x)
    combine(wcb, r3b, s4b, y)

    cr_copy.wait_recv()
    served_all = crk[0] + crk[1]
    mine = (iota((8, 128), 0) == a) & (iota((8, 128), 1) == c)
    copy_rows[0] = jnp.sum(jnp.where(mine, served_all, 0.0)).astype(jnp.int32)

    s_landed()
    for landed, own, finals, me, first in ((a_landed, s4a, r4a, x, 0), (b_landed, s4b, r4b, y, 1024)):
        landed()

        def total(n, _):
            cols = pl.ds(pl.multiple_of(n * 256, 256), 256)
            wide_cols = pl.ds(pl.multiple_of(first + n * 256, 256), 256)
            v = hid[:, wide_cols] + sp[a, :, wide_cols].astype(F32) + own[me, :, cols].astype(F32)
            for i in range(2):
                v = v + sr[i, :, wide_cols].astype(F32) + finals[i, :, cols].astype(F32)
            out[:, wide_cols] = v[0:124].astype(BF)
            return 0

        lax.fori_loop(0, 4, total, 0)
    for copy in sent:
        if id(copy) not in finished:
            copy.wait_send()


def body(
    attn_prefill, decode_held, decode_source, residual, live_rows, expert_ids, replica_pick, w_out, norm_gain, router,
    exp_gate, exp_up, exp_down, shared_gate, shared_up, shared_down,
):
    vmem = pl.BlockSpec(memory_space=pltpu.VMEM)
    smem = pl.BlockSpec(memory_space=pltpu.SMEM)
    hbm = pl.BlockSpec(memory_space=pl.ANY)
    V = pltpu.VMEM
    return pl.pallas_call(
        kernel,
        out_shape=(jax.ShapeDtypeStruct((124, 2048), BF), jax.ShapeDtypeStruct((1,), jnp.int32)),
        in_specs=[vmem, vmem, smem, vmem, smem, vmem, vmem, hbm, vmem, vmem, hbm, hbm, hbm, hbm, hbm, hbm],
        out_specs=(vmem, smem),
        scratch_shapes=[
            V((2048, 512), BF), V((2048, 1408), BF), V((2048, 1408), BF), V((1408, 2048), BF),
            V((352, 2048), BF), V((352, 2048), BF), V((352, 2048), BF),
            V((128, 2048), F32), V((3, 128, 2048), BF), V((2, 128, 512), BF), V((4, 128, 512), BF),
            V((16, 512), F32), V((16, 512), BF), V((4, 16, 512), BF),
            V((2, 4, 4, 128, 128), BF), V((2, 4, 4, 128, 128), BF),
            V((8, 128), jnp.int32), V((32, 128), F32), V((32, 128), F32), V((4, 8, 128), F32), V((4, 8, 128), F32),
            V((8, 128), F32), V((4, 8, 128), F32), V((4, 8, 128), F32), V((4, 8, 128), F32), V((2, 8, 128), F32),
            V((3, 8, 128), F32),
            V((32, 128), F32), V((32, 128), F32), V((4, 8, 128), F32), V((4, 8, 128), F32),
            V((4, 128, 1024), BF), V((4, 128, 1024), BF),
            V((4, 128, 2048), BF), V((4, 128, 2048), BF), V((2, 64, 2048), BF), V((2, 128, 2048), BF),
            V((384, 512), BF),
            V((2, 4, 96, 1024), BF), V((2, 4, 96, 1024), BF), V((2, 4, 96, 1024), BF), V((2, 4, 96, 1024), BF),
            V((384, 1408), BF), V((384, 1408), BF),
            V((2, 4, 96, 1024), BF), V((2, 4, 96, 1024), BF),
            V((768, 512), F32), V((512, 768), BF), V((512, 768), BF),
            V((4, 128, 1024), BF), V((4, 128, 1024), BF), V((2, 64, 1024), BF), V((2, 64, 1024), BF),
            V((2, 128, 1024), BF), V((2, 128, 1024), BF),
            pltpu.SemaphoreType.DMA((COPIES,)), pltpu.SemaphoreType.DMA((COPIES,)),
            pltpu.SemaphoreType.DMA((7,)), pltpu.SemaphoreType.DMA((4,)),
        ],
        compiler_params=pltpu.CompilerParams(collective_id=0, has_side_effects=True, vmem_limit_bytes=62 << 20),
        cost_estimate=pl.CostEstimate(flops=17_000_000_000, bytes_accessed=26_000_000, transcendentals=2_000_000),
        name="moe",
    )(
        attn_prefill, decode_held, decode_source, residual, live_rows, expert_ids.T, replica_pick, w_out,
        norm_gain.reshape(1, 2048), router.T, exp_gate, exp_up, exp_down, shared_gate, shared_up, shared_down,
    )


def solution(mesh):
    rows = P(("dp", "expert"), None)
    flat = P(("dp", "expert"))
    placed = (
        rows, rows, flat, rows, flat, rows, rows, P(None, "dp"), P(), P(),
        P("expert", None, None), P("expert", None, None), P("expert", None, None),
        P("dp", None), P("dp", None), P("dp", None),
    )
    return jax.shard_map(body, mesh=mesh, in_specs=placed, out_specs=(rows, flat), check_vma=False)
```

time: 122 us -> 104 us (0.85)
  Pallas kernels: 117 us -> 98.4 us
    pallas_call x1, Pallas kernels: 117 us -> 98.4 us  [body(): pl.pallas_call(kernel, out_shape=(jax.ShapeDtypeStruct((124, 2048), BF),...]
where the time goes in v2:
time: 104 us; the launch traced here: 103 us
  Pallas kernels  98.4 us (95%)
  between operations  2.99 us (3%)
  local copies, waits for them, and re-layouts  1.88 us (2%)
    pallas_call x1, Pallas kernels, body(): pl.pallas_call(kernel, out_shape=(jax.ShapeDtypeStruct((124, 2048), BF),...  98.4 us

profile of v2, /device:TPU:1, one launch (start us, length us, event | category | flops | bytes accessed | tf_op | source)
XLA Modules:
  0.0 103.3 jit_solution(10772661350288826057)
XLA Ops:
  1.3 98.4 %moe.1 = (bf16[124,2048]{1,0:T(8,128)(2,1)}, s32[1]{0:T(128)}) custom-call(bf16[120,2048]{1,0:T(8,128)(2,1)} %pre.1, bf16[4,2048]{1,0:T(4,128)(2,1)} %held.1, s32[4]{0:T(128)} %source.1, bf16[124,2048]{1,0:T(8,128)(2,1)} %resid.1, s32[1]{0:T(128)S(6)} %copy.20.live, s32[6,124]{1,0:T(8,128)} %bitcast.5, s32[1,32]{1,0:T(1,128)} %pick.1, ...), custom_call_target="tpu_custom_call" | custom-call | flops 16999999488 | bytes 26000000 | tf_op jit(solution)/shard_map/moe/pallas_call | solution.py:491
  99.7 1.9 %copy.21 = bf16[124,2048]{1,0:T(8,128)(2,1)} copy(bf16[124,2048]{1,0:T(8,128)(2,1)} %get-tuple-element.4) | data formatting | bytes 1015808

commit v3 on v2

--- a/solution.py
+++ b/solution.py
@@ -14,7 +14,7 @@
 NT = (((1,), (1,)), ((), ()))
 
 GROUPS = dict(
-    Z_TOP=2, Z_BOTTOM=2, Z_RET=2, HELD=3, W_PIECE=2, WA_X=6, WA_Y=6, WB_Y=6, WB_X=6, W_CORE=2, CODE_A=3, CODE_B=3, CR_Z=3,
+    Z_TOP=2, Z_BOTTOM=2, Z_RET=4, HELD=3, W_PIECE=2, WA_X=3, WA_Y=3, WB_Y=3, WB_X=3, W_CORE=8, CODE_A=3, CODE_B=3, CR_Z=3,
     CR_X=3, CR_Y=3, CR_K=1, PROB_A=3, PROB_B=3, X_AG=6, Y_AG=6, S_AG=6, DIS_A=8, DIS_B=8, S_SUM=6, RET_A=8, RET_B=8, SUM_A=6, SUM_B=6,
 )
 COPIES = sum(GROUPS.values())
@@ -155,11 +155,38 @@
     for load in loads[1:]:
         load.start()
 
+    row64, col64 = iota((64, 64), 0), iota((64, 64), 1)
+    chosen = jnp.full((64, 64), -64, jnp.int32)
+    for i in range(4):
+        chosen = jnp.where(row64 == 56 + i, source[i] // 4 * 16 + lax.rem(source[i], 4), chosen)
+    for copy in pieces:
+        copy.wait_recv()
+    ax_copies = others(x, ID["WA_X"], xdev, lambda i: wo_a.at[k, y, x], lambda i: wo_a.at[k, y, x])
+    by_copies = others(y, ID["WB_Y"], ydev, lambda i: wo_b.at[k, x, y], lambda i: wo_b.at[k, x, y])
+    for copy in held_copies:
+        copy.wait_recv()
+    for i in range(4):
+        cols = slice(512 * i, 512 * i + 512)
+        picked = dot(jnp.where(col64 == chosen + 4 * i, 1.0, 0.0).astype(BF), held_all[...].reshape(64, 512))
+        zb[0, 64:128, cols] = (hid[64:128, cols] + picked).astype(BF)
+    bottoms = both(ID["Z_BOTTOM"], bottom)
+    for copy in ax_copies:
+        copy.wait_recv()
+    ay_copies = others(y, ID["WA_Y"], ydev, lambda i: wo_a.at[k, y], lambda i: wo_a.at[k, y])
+    for copy in by_copies:
+        copy.wait_recv()
+    bx_copies = others(x, ID["WB_X"], xdev, lambda i: wo_b.at[k, x], lambda i: wo_b.at[k, x])
+
+    def to_sibling(i, wo, slot):
+        return send(ID["W_CORE"] + i, wo.at[k, slot], wo.at[k, slot], at(a, x, y, 1 - k))
+
+    core_copies = [to_sibling(0, wo_a, y), to_sibling(4, wo_b, x)]
+
     idsp[...] = jnp.full((8, 128), -1, jnp.int32)
     idsp[0:6, 0:124] = ids[...]
     lane = iota((32, 128), 1)
     row = iota((32, 128), 0)
-    alive = (lane < live[0]) | (lane >= 120)
+    alive = (lane < live[...]) | (lane >= 120)
     before = jnp.where(iota((128, 128), 0) < iota((128, 128), 1), 1.0, 0.0).astype(BF)
 
     def match(expert):
@@ -192,54 +219,37 @@
     crz[a] = svt[...]
     cr_copies = others(a, ID["CR_Z"], zdev, lambda i: svt, lambda i: crz.at[a])
 
-    row64, col64 = iota((64, 64), 0), iota((64, 64), 1)
-    chosen = jnp.full((64, 64), -64, jnp.int32)
-    for i in range(4):
-        chosen = jnp.where(row64 == 56 + i, source[i] // 4 * 16 + lax.rem(source[i], 4), chosen)
-    for copy in held_copies:
-        copy.wait_recv()
-    for i in range(4):
-        cols = slice(512 * i, 512 * i + 512)
-        picked = dot(jnp.where(col64 == chosen + 4 * i, 1.0, 0.0).astype(BF), held_all[...].reshape(64, 512))
-        zb[0, 64:128, cols] = (hid[64:128, cols] + picked).astype(BF)
-    bottoms = both(ID["Z_BOTTOM"], bottom)
-    for copy in pieces:
-        copy.wait_recv()
-    ax_copies, ax_forward = ring(ID["WA_X"], wo_a.at[k, y], x, xdev)
-    by_copies, by_forward = ring(ID["WB_Y"], wo_b.at[k, x], y, ydev)
     pr[a] = dot(zb[0], w_out[...]).astype(BF)
-    ax_forward()
-    by_forward()
-    for copy in ax_copies[2:]:
-        copy.wait_recv()
-    ay_copies, ay_forward = ring(ID["WA_Y"], wo_a.at[k], y, ydev, 2)
-    for copy in by_copies[2:]:
-        copy.wait_recv()
-    bx_copies, bx_forward = ring(ID["WB_X"], wo_b.at[k], x, xdev, 2)
-    ay_forward()
-    bx_forward()
-    for copy in ay_copies[2:]:
-        copy.wait_recv()
-    core_copies = [send(ID["W_CORE"], wo_a.at[k], wo_a.at[k], at(a, x, y, 1 - k))]
-    for copy in bx_copies[2:]:
-        copy.wait_recv()
-    core_copies += [send(ID["W_CORE"] + 1, wo_b.at[k], wo_b.at[k], at(a, x, y, 1 - k))]
     returns = []
-    for i, slot in enumerate((left, right)):
-        tops[i].wait_recv()
-        bottoms[i].wait_recv()
-        pb[i] = dot(zb[1 + i], w_out[...]).astype(BF)
-        returns.append(send(ID["Z_RET"] + i, pb.at[i], pr.at[a], zdev(slot)))
+
+    def project(i, copies, part):
+        for copy in copies:
+            copy.wait_recv()
+        rows = jnp.concatenate([zb[1, part, :], zb[2, part, :]], axis=0)
+        pb[i] = dot(rows, w_out[...]).astype(BF)
+        returns.append(send(ID["Z_RET"] + 2 * i, pb.at[i, top], pr.at[a, part], zdev(left)))
+        returns.append(send(ID["Z_RET"] + 2 * i + 1, pb.at[i, bottom], pr.at[a, part], zdev(right)))
+
+    project(0, tops, top)
+    for i in (1, 2, 3):
+        ay_copies[i - 1].wait_recv()
+        core_copies.append(to_sibling(i, wo_a, m4(y + 4 - i)))
+        bx_copies[i - 1].wait_recv()
+        core_copies.append(to_sibling(4 + i, wo_b, m4(x + 4 - i)))
+    project(1, bottoms, bottom)
+
+    def far(core):
+        v = jnp.zeros((128, 256), F32)
+        for i in range(8):
+            m, n = i // 2, i % 2 * 2
+            rows = [jnp.concatenate([wo_a[core, j, m], wo_b[core, m, j]], axis=1) for j in (n, n + 1)]
+            v = v + dot(zb[0, :, 256 * i : 256 * i + 256], jnp.concatenate(rows, axis=0))
+        pr[opposite, :, pl.ds(pl.multiple_of(core * 256, 256), 256)] = v.astype(BF)
+
+    far(k)
     for copy in core_copies:
         copy.wait_recv()
-    far = jnp.zeros((128, 512), F32)
-    for i in range(8):
-        rows = [
-            jnp.concatenate([wo_a[0, n, m], wo_b[0, m, n], wo_a[1, n, m], wo_b[1, m, n]], axis=1)
-            for m, n in ((i // 2, i % 2 * 2), (i // 2, i % 2 * 2 + 1))
-        ]
-        far = far + dot(zb[0, :, 256 * i : 256 * i + 256], jnp.concatenate(rows, axis=0))
-    pr[opposite] = far.astype(BF)
+    far(1 - k)
 
     for copy in cr_copies:
         copy.wait_recv()
@@ -292,6 +302,30 @@
     for copy in code_copies:
         copy.wait_recv()
 
+    for load in loads[1:4]:
+        load.wait()
+
+    def shared(i):
+        rows = sb[i]
+        gate = lax.dot_general(rows, sg[...], NT, preferred_element_type=F32)
+        up = lax.dot_general(rows, su[...], NT, preferred_element_type=F32)
+        hidden_units = (gate / (1.0 + jnp.exp(-gate)) * up).astype(BF)
+
+        def columns(n, _):
+            cols = pl.ds(pl.multiple_of(n * 512, 512), 512)
+            sp[i, :, cols] = dot(hidden_units, sd[:, cols]).astype(BF)
+            return 0
+
+        lax.fori_loop(0, 4, columns, 0, unroll=True)
+
+    def shared_of(i, parts):
+        for part in parts:
+            s_copies[part].wait_recv()
+        shared(m4(a + i))
+
+    s_far, s_right, s_left, s_pass, s_landed = ring_sum(ID["S_SUM"], sp, s_mid, sr, a, zdev)
+    shared(a)
+
     slot96 = iota((96, 512), 0).astype(F32)
 
     def codes(ref, i):
@@ -310,69 +344,46 @@
             return 0
 
         lax.fori_loop(0, 4, columns, 0, unroll=True)
-        copies = []
-        for i in range(4):
+
+        def start(i):
             to = m4(me + i)
             if step == 0 and i == 0:
                 copy = pltpu.make_async_copy(slots.at[core, to], landing.at[k, me], ls.at[base])
                 copy.start()
                 locals_.append(copy)
-                continue
-            copies.append(send(group + 4 * step + i, slots.at[core, to], landing.at[k, me], dev(to, core)))
-        return copies
+            else:
+                arrive[step].append(send(group + 4 * step + i, slots.at[core, to], landing.at[k, me], dev(to, core)))
+
+        return start
 
     col_dev = lambda i, core: at(a, x, i, core)
     row_dev = lambda i, core: at(a, i, y, core)
     for copy in x_copies[2:]:
         copy.wait_recv()
     arrive = [[], []]
-    arrive[0] += dispatch(0, 0, k, ca, buf_a, s2a, r2a, y, col_dev, ID["DIS_A"])
+    first_a = dispatch(0, 0, k, ca, buf_a, s2a, r2a, y, col_dev, ID["DIS_A"])
+    for i in range(4):
+        first_a(i)
     for copy in y_copies[2:]:
         copy.wait_recv()
-    arrive[0] += dispatch(1, 0, k, cb, buf_b, s2b, r2b, x, row_dev, ID["DIS_B"])
-    arrive[1] += dispatch(0, 1, 1 - k, ca, buf_a, s2a, r2a, y, col_dev, ID["DIS_A"])
-    arrive[1] += dispatch(1, 1, 1 - k, cb, buf_b, s2b, r2b, x, row_dev, ID["DIS_B"])
-
-    for load in loads[1:4]:
-        load.wait()
-
-    def shared(i):
-        rows = sb[i]
-        gate = lax.dot_general(rows, sg[...], NT, preferred_element_type=F32)
-        up = lax.dot_general(rows, su[...], NT, preferred_element_type=F32)
-        hidden_units = (gate / (1.0 + jnp.exp(-gate)) * up).astype(BF)
-
-        def columns(n, _):
-            cols = pl.ds(pl.multiple_of(n * 512, 512), 512)
-            sp[i, :, cols] = dot(hidden_units, sd[:, cols]).astype(BF)
-            return 0
-
-        lax.fori_loop(0, 4, columns, 0, unroll=True)
-
-    def shared_of(i, parts):
-        for part in parts:
-            s_copies[part].wait_recv()
-        shared(m4(a + i))
-
-    s_far, s_right, s_left, s_pass, s_landed = ring_sum(ID["S_SUM"], sp, s_mid, sr, a, zdev)
-    shared(a)
+    first_b = dispatch(1, 0, k, cb, buf_b, s2b, r2b, x, row_dev, ID["DIS_B"])
+    for i in range(4):
+        first_b(i)
+    second_a = dispatch(0, 1, 1 - k, ca, buf_a, s2a, r2a, y, col_dev, ID["DIS_A"])
+    second_b = dispatch(1, 1, 1 - k, cb, buf_b, s2b, r2b, x, row_dev, ID["DIS_B"])
+    second_a(0)
+    second_b(0)
+
     shared_of(3, (2,))
     s_left()
     shared_of(1, (3,))
     s_right()
 
-    for copy in prob_copies:
-        copy.wait_recv()
-
-    def weights(code, prob, into):
-        for i in range(8):
-            e = lax.rem(i, 4) * 2 + i // 4
-            hit = slot96 == codes(code, e)
-            wide[96 * i : 96 * i + 96, :] = jnp.where(hit, codes(prob, e), 0.0)
-        into[...] = wide[...].T.astype(BF)
-
-    weights(ca, pa, wca)
-    weights(cb, pb_b, wcb)
+    for i in (1, 2, 3):
+        for copy, second in ((arrive[0][i - 1], second_a), (arrive[0][i + 2], second_b)):
+            copy.wait_send()
+            finished.add(id(copy))
+            second(i)
 
     for copy in cr_copies:
         copy.wait_recv()
@@ -406,8 +417,9 @@
         for first in range(0, 1408, 256):
             up(slice(first, min(first + 256, 1408)))
         for copy in arrive[step]:
-            copy.wait_send()
-            finished.add(id(copy))
+            if id(copy) not in finished:
+                copy.wait_send()
+                finished.add(id(copy))
         copies = []
         for group, inner, slots, landing, me, dev, first in (
             (ID["RET_A"], inner_a, s2a, r3a, y, col_dev, 0),
@@ -428,11 +440,25 @@
         return copies
 
     back = expert(0, k)
+    back += expert(1, 1 - k)
     shared_of(2, (4, 5))
     s_far()
-    back += expert(1, 1 - k)
+    back_a, back_b = [back[i] for i in (0, 1, 2, 6, 7, 8, 9)], [back[i] for i in (3, 4, 5, 10, 11, 12, 13)]
+
+    for copy in prob_copies:
+        copy.wait_recv()
+
+    def weights(code, prob, into):
+        for i in range(8):
+            e = lax.rem(i, 4) * 2 + i // 4
+            hit = slot96 == codes(code, e)
+            wide[96 * i : 96 * i + 96, :] = jnp.where(hit, codes(prob, e), 0.0)
+        into[...] = wide[...].T.astype(BF)
+
+    weights(ca, pa, wca)
+    weights(cb, pb_b, wcb)
+
     s_pass()
-    back_a, back_b = [back[i] for i in (0, 1, 2, 6, 7, 8, 9)], [back[i] for i in (3, 4, 5, 10, 11, 12, 13)]
 
     def combine(wc, landed, sums, i):
         rows = pl.ds(pl.multiple_of(i * 128, 128), 128)
@@ -491,7 +517,7 @@
     return pl.pallas_call(
         kernel,
         out_shape=(jax.ShapeDtypeStruct((124, 2048), BF), jax.ShapeDtypeStruct((1,), jnp.int32)),
-        in_specs=[vmem, vmem, smem, vmem, smem, vmem, vmem, hbm, vmem, vmem, hbm, hbm, hbm, hbm, hbm, hbm],
+        in_specs=[vmem, vmem, smem, vmem, vmem, vmem, vmem, hbm, vmem, vmem, hbm, hbm, hbm, hbm, hbm, hbm],
         out_specs=(vmem, smem),
         scratch_shapes=[
             V((2048, 512), BF), V((2048, 1408), BF), V((2048, 1408), BF), V((1408, 2048), BF),
@@ -519,7 +545,7 @@
         cost_estimate=pl.CostEstimate(flops=17_000_000_000, bytes_accessed=26_000_000, transcendentals=2_000_000),
         name="moe",
     )(
-        attn_prefill, decode_held, decode_source, residual, live_rows, expert_ids.T, replica_pick, w_out,
+        attn_prefill, decode_held, decode_source, residual, live_rows.reshape(1, 1), expert_ids.T, replica_pick, w_out,
         norm_gain.reshape(1, 2048), router.T, exp_gate, exp_up, exp_down, shared_gate, shared_up, shared_down,
     )
 

time: 104 us -> 100 us (0.962)
  Pallas kernels: 98.4 us -> 93.7 us
    pallas_call x1, Pallas kernels: 98.4 us -> 93.7 us  [body(): pl.pallas_call(kernel, out_shape=(jax.ShapeDtypeStruct((124, 2048), BF),...]
where the time goes in v3:
time: 100 us; the launch traced here: 98.5 us
  Pallas kernels  93.7 us (94%)
  between operations  2.99 us (3%)
  local copies, waits for them, and re-layouts  1.88 us (2%)
    pallas_call x1, Pallas kernels, body(): pl.pallas_call(kernel, out_shape=(jax.ShapeDtypeStruct((124, 2048), BF),...  93.7 us

profile of v3, /device:TPU:1, one launch (start us, length us, event | category | flops | bytes accessed | tf_op | source)
XLA Modules:
  0.0 98.5 jit_solution(567135968623811526)
XLA Ops:
  1.3 93.7 %moe.1 = (bf16[124,2048]{1,0:T(8,128)(2,1)}, s32[1]{0:T(128)}) custom-call(bf16[120,2048]{1,0:T(8,128)(2,1)} %pre.1, bf16[4,2048]{1,0:T(4,128)(2,1)} %held.1, s32[4]{0:T(128)} %source.1, bf16[124,2048]{1,0:T(8,128)(2,1)} %resid.1, s32[1,1]{1,0:T(1,128)} %bitcast.4.live, s32[6,124]{1,0:T(8,128)} %bitcast.7, s32[1,32]{1,0:T(1,128)} %pick.1, ...), custom_call_target="tpu_custom_call" | custom-call | flops 16999999488 | bytes 26000000 | tf_op jit(solution)/shard_map/moe/pallas_call | solution.py:517
  95.0 1.9 %copy.21 = bf16[124,2048]{1,0:T(8,128)(2,1)} copy(bf16[124,2048]{1,0:T(8,128)(2,1)} %get-tuple-element.4) | data formatting | bytes 1015808

commit v4 on v3

--- a/solution.py
+++ b/solution.py
@@ -128,9 +128,7 @@
 
     left, right, opposite = m4(a + 3), m4(a + 1), m4(a + 2)
     top, bottom = pl.ds(0, 64), pl.ds(64, 64)
-    hid[0:120, :] = pre[...].astype(F32)
-    hid[120:128, :] = jnp.zeros((8, 2048), F32)
-    zb[0, 0:64, :] = hid[0:64, :].astype(BF)
+    zb[0, 0:64, :] = pre[0:64, :]
     for i in range(4):
         held_f[4 * i : 4 * i + 4, :] = held[:, 512 * i : 512 * i + 512].astype(F32)
     held_s[...] = held_f[...].astype(BF)
@@ -155,6 +153,8 @@
     for load in loads[1:]:
         load.start()
 
+    hid[0:120, :] = pre[...].astype(F32)
+    hid[120:128, :] = jnp.zeros((8, 2048), F32)
     row64, col64 = iota((64, 64), 0), iota((64, 64), 1)
     chosen = jnp.full((64, 64), -64, jnp.int32)
     for i in range(4):
@@ -231,6 +231,13 @@
         returns.append(send(ID["Z_RET"] + 2 * i + 1, pb.at[i, bottom], pr.at[a, part], zdev(right)))
 
     project(0, tops, top)
+    hid[120:128, :] = jnp.zeros((8, 2048), F32)
+    hid[0:124, :] = resid[...].astype(F32)
+    for copy in cr_copies:
+        copy.wait_recv()
+    crs[0] = crz[0] + crz[1] + crz[2] + crz[3]
+    crx[x] = crs[0]
+    cr_copies = others(x, ID["CR_X"], xdev, lambda i: crs.at[0], lambda i: crx.at[x])
     for i in (1, 2, 3):
         ay_copies[i - 1].wait_recv()
         core_copies.append(to_sibling(i, wo_a, m4(y + 4 - i)))
@@ -251,14 +258,6 @@
         copy.wait_recv()
     far(1 - k)
 
-    for copy in cr_copies:
-        copy.wait_recv()
-    crs[0] = crz[0] + crz[1] + crz[2] + crz[3]
-    crx[x] = crs[0]
-    cr_copies = others(x, ID["CR_X"], xdev, lambda i: crs.at[0], lambda i: crx.at[x])
-
-    hid[120:128, :] = jnp.zeros((8, 2048), F32)
-    hid[0:124, :] = resid[...].astype(F32)
     for copy in returns:
         copy.wait_recv()
     for i in range(4):

time: 100 us -> 101 us (1.010)
  Pallas kernels: 93.7 us -> 95.2 us
    pallas_call x1, Pallas kernels: 93.7 us -> 95.2 us  [body(): pl.pallas_call(kernel, out_shape=(jax.ShapeDtypeStruct((124, 2048), BF),...]
where the time goes in v4:
time: 101 us; the launch traced here: 100 us
  Pallas kernels  95.2 us (94%)
  between operations  2.99 us (3%)
  local copies, waits for them, and re-layouts  1.88 us (2%)
    pallas_call x1, Pallas kernels, body(): pl.pallas_call(kernel, out_shape=(jax.ShapeDtypeStruct((124, 2048), BF),...  95.2 us

profile of v4, /device:TPU:1, one launch (start us, length us, event | category | flops | bytes accessed | tf_op | source)
XLA Modules:
  0.0 100.0 jit_solution(14075048317646086996)
XLA Ops:
  1.3 95.2 %moe.1 = (bf16[124,2048]{1,0:T(8,128)(2,1)}, s32[1]{0:T(128)}) custom-call(bf16[120,2048]{1,0:T(8,128)(2,1)} %pre.1, bf16[4,2048]{1,0:T(4,128)(2,1)} %held.1, s32[4]{0:T(128)} %source.1, bf16[124,2048]{1,0:T(8,128)(2,1)} %resid.1, s32[1,1]{1,0:T(1,128)} %bitcast.4.live, s32[6,124]{1,0:T(8,128)} %bitcast.7, s32[1,32]{1,0:T(1,128)} %pick.1, ...), custom_call_target="tpu_custom_call" | custom-call | flops 16999999488 | bytes 26000000 | tf_op jit(solution)/shard_map/moe/pallas_call | solution.py:516
  96.5 1.9 %copy.21 = bf16[124,2048]{1,0:T(8,128)(2,1)} copy(bf16[124,2048]{1,0:T(8,128)(2,1)} %get-tuple-element.4) | data formatting | bytes 1015808
